TPU v7x, 768 devices: a whole 4x8x12 slice. The times are simulated.
768 devices in a mesh: dp: 48 (over z, y_hi, core), mp: 16 (over y_lo, x).
Axes of the slice: x: 4, y: 8 (y_hi: 2, y_lo: 4; y = y_hi * 4 + y_lo), z: 12, core: 2. Of those that a mesh axis runs over, the one named last changes fastest.
Arguments:
- hidden: bfloat16 [768, 64, 1152], P('dp', None, 'mp'), may hold values from -6 to 6
- counts: int32 [768], P('dp'), may hold values from 1 to 64, as said below
- w_qkv: bfloat16 [1152, 3456], P(None, 'mp')
- w_out: bfloat16 [1152, 1152], P('mp'), may hold values from -0.1875 to 0.1875
- images: float32 [768, 1152], P('dp'), may hold values from -0.1875 to 0.1875
- logit_params: float32 [2], replicated, may hold values from -0.5 to 2.5
Outputs:
- grad_qkv: float32 [1152, 3456], P('dp', 'mp')
- grad_out: float32 [1152, 1152], P('mp', 'dp')
Inputs may be any that keep to these rules, and one draw needn't show every extreme that they name: `counts`: each caption has 1 to 64 real tokens; padding follows them.
All inputs are finite; a program needn't handle non-finite values.
Results may differ from a plain program's by a relative error of at most 0.012.
Values may be sent and summed in bfloat16 or wider, within the bound.
A program may use at most 32 MiB of HBM per device.

v0:
```python
import jax
import jax.numpy as jnp
from jax import lax
from jax.sharding import PartitionSpec as P

HD = 72


def layer_norm(tokens):
    values = tokens.astype(jnp.float32)
    center = jnp.mean(values, axis=-1, keepdims=True)
    spread = jnp.mean((values - center) ** 2, axis=-1, keepdims=True)
    return ((values - center) * lax.rsqrt(spread + 1e-06)).astype(jnp.bfloat16)


def pair_terms(text_emb, text_ids, incoming, image_ids, logit_scale, logit_bias):
    logits = (
        logit_scale * jnp.dot(text_emb, incoming.T, precision=lax.Precision.HIGHEST) + logit_bias
    )
    labels = jnp.where(text_ids[:, None] == image_ids[None, :], 1.0, -1.0).astype(jnp.float32)
    weight = -labels * jax.nn.sigmoid(-labels * logits)
    return jnp.dot(weight, incoming, precision=lax.Precision.HIGHEST)


def on_device(hidden, counts, w_qkv, w_out, images, logit_params):
    gathered = lax.all_gather(hidden, "mp", axis=2, tiled=True)
    n_caps, length, n_width = gathered.shape
    heads_here = w_out.shape[0] // HD
    live_mask = jnp.arange(length, dtype=jnp.int32)[None, :] < counts[:, None]
    live_float = live_mask.astype(jnp.float32)
    inv_count = 1.0 / counts.astype(jnp.float32)
    normed = layer_norm(gathered)
    flat_normed = normed.reshape(n_caps * length, n_width)
    packed = jnp.dot(flat_normed, w_qkv, preferred_element_type=jnp.float32)
    packed = packed.astype(jnp.bfloat16).reshape(n_caps, length, heads_here, 3, HD)
    queries = packed[:, :, :, 0, :]
    key_vecs = packed[:, :, :, 1, :]
    values = packed[:, :, :, 2, :]
    scale_inv = 1.0 / jnp.sqrt(jnp.float32(HD))
    scores = (
        jnp.einsum("clhe,cmhe->chlm", queries, key_vecs, preferred_element_type=jnp.float32)
        * scale_inv
    )
    key_live = live_mask[:, None, None, :]
    top = jnp.max(jnp.where(key_live, scores, -jnp.inf), axis=-1, keepdims=True)
    expo = jnp.where(key_live, jnp.exp(scores - top), 0.0)
    attn_probs = expo / jnp.sum(expo, axis=-1, keepdims=True)
    attn_out = jnp.einsum(
        "chlm,cmhe->clhe",
        attn_probs.astype(jnp.bfloat16),
        values,
        preferred_element_type=jnp.float32,
    ).astype(jnp.bfloat16)
    live_bf = live_mask.astype(jnp.bfloat16)
    pooled_mix = jnp.einsum("cl,clhe->che", live_bf, attn_out, preferred_element_type=jnp.float32)
    pooled_mix = pooled_mix.reshape(n_caps, heads_here * HD) * inv_count[:, None]
    pooled_hid = (
        jnp.einsum("cl,cld->cd", live_bf, gathered, preferred_element_type=jnp.float32)
        * inv_count[:, None]
    )
    out_f = w_out.astype(jnp.float32)
    attn_term = jnp.dot(pooled_mix, out_f, precision=lax.Precision.HIGHEST)
    pooled = lax.psum(attn_term.astype(jnp.bfloat16), "mp").astype(jnp.float32) + pooled_hid
    inv_norm = lax.rsqrt(jnp.sum(pooled * pooled, axis=-1, keepdims=True) + 1e-06)
    text_emb = pooled * inv_norm
    logit_scale = jnp.exp(logit_params[0])
    logit_bias = logit_params[1]
    text_ids = lax.axis_index("dp") * n_caps + jnp.arange(n_caps, dtype=jnp.int32)
    empty = jnp.zeros((n_caps, n_width), jnp.float32)
    incoming = lax.all_gather(images.astype(jnp.bfloat16), "dp", axis=0, tiled=True).astype(
        jnp.float32
    )
    image_ids = jnp.arange(incoming.shape[0], dtype=jnp.int32)
    pulled = empty + pair_terms(text_emb, text_ids, incoming, image_ids, logit_scale, logit_bias)
    text_grad = logit_scale * pulled
    along = jnp.sum(text_emb * text_grad, axis=-1, keepdims=True)
    pooled_grad = (text_grad - text_emb * along) * inv_norm
    grad_o = jnp.dot(pooled_mix.T, pooled_grad, precision=lax.Precision.HIGHEST)
    per_caption = (
        jnp.dot(pooled_grad, out_f.T, precision=lax.Precision.HIGHEST) * inv_count[:, None]
    )
    per_caption = per_caption.reshape(n_caps, heads_here, HD)
    upstream = live_float[:, :, None, None] * per_caption[:, None, :, :]
    query_f = queries.astype(jnp.float32)
    key_f = key_vecs.astype(jnp.float32)
    value_f = values.astype(jnp.float32)
    prob_grad = jnp.einsum("clhe,cmhe->chlm", upstream, value_f, precision=lax.Precision.HIGHEST)
    value_grad = jnp.einsum(
        "chlm,clhe->cmhe", attn_probs, upstream, precision=lax.Precision.HIGHEST
    )
    score_grad = attn_probs * (prob_grad - jnp.sum(attn_probs * prob_grad, axis=-1, keepdims=True))
    query_grad = (
        jnp.einsum("chlm,cmhe->clhe", score_grad, key_f, precision=lax.Precision.HIGHEST)
        * scale_inv
    )
    key_grad = (
        jnp.einsum("chlm,clhe->cmhe", score_grad, query_f, precision=lax.Precision.HIGHEST)
        * scale_inv
    )
    qkv_grad = jnp.stack([query_grad, key_grad, value_grad], axis=3).astype(jnp.bfloat16)
    qkv_grad = qkv_grad.reshape(n_caps * length, 3 * heads_here * HD)
    grad_in = jnp.einsum("nd,nf->df", flat_normed, qkv_grad, preferred_element_type=jnp.float32)
    grad_qkv, grad_out = (
        lax.psum_scatter(grad_in, "dp", scatter_dimension=0, tiled=True),
        lax.psum_scatter(grad_o, "dp", scatter_dimension=1, tiled=True),
    )
    return (grad_qkv, grad_out)


def solution(mesh):
    placed = (P("dp", None, "mp"), P("dp"), P(None, "mp"), P("mp", None), P("dp", None), P())
    return jax.shard_map(
        on_device,
        mesh=mesh,
        in_specs=placed,
        out_specs=(P("dp", "mp"), P("mp", "dp")),
        check_vma=False,
    )
```

profile of v0, /device:TPU:1, one launch (start us, length us, event | category | flops | bytes accessed | tf_op | source)
XLA Modules:
  0.0 592.0 jit_solution(2781649940563270673)
XLA Ops:
  7.2 2.0 copy.26
  9.3 1.5 convert_element_type.77
  10.8 1.3 fusion.51
  12.2 1.2 convert_divide_fusion
  13.3 1.3 fusion.63
  15.9 88.3 %all-gather.3.cloned.1.call-done = bf16[16,64,1152]{1,0,2:T(8,128)(2,1)} async-done(((bf16[16,64,72]{1,0,2:T(8,128)(2,1)}), bf16[16,64,1152]{1,0,2:T(8,128)(2,1)}) %all-gather.3.cloned.1.call-update) | async-done | bytes 2359312 | tf_op jit(solution)/shard_map/all_gather | solution.py:26
  104.2 6.0 %copy.27 = bf16[16,64,1152]{2,1,0:T(8,128)(2,1)S(1)} copy(bf16[16,64,1152]{1,0,2:T(8,128)(2,1)} %all-gather.3.cloned.1.call-done) | data formatting | bytes 4718592 | tf_op jit(solution)/shard_map/all_gather | solution.py:26
  112.0 1.4 copy-done.1
  114.4 1.5 reshape.218
  115.9 2.0 fusion.62
  117.9 1.9 copy.39
  119.8 1.0 copy.40
  120.8 1.0 copy.41
  121.8 1.3 convolution_multiply_fusion.1
  123.1 2.5 fusion.64
  125.6 2.2 fusion.12
  128.8 64.0 %psum.7 = bf16[16,1152]{1,0:T(8,128)(2,1)S(1)} all-reduce(bf16[16,1152]{1,0:T(8,128)(2,1)S(1)} %convolution_convert_fusion), channel_id=1, replica_groups=mesh['dp'=48,'mp'=16] {'mp'}, use_global_device_ids=true, to_apply=%region_4.5 | all-reduce | flops 18432 | bytes 73728 | tf_op jit(solution)/shard_map/psum | solution.py:63
  193.5 44.3 %all-gather.5.cloned.1.call-done = bf16[768,1152]{1,0:T(8,128)(2,1)} async-done(((bf16[16,1152]{1,0:T(8,128)(2,1)}), bf16[768,1152]{1,0:T(8,128)(2,1)}) %all-gather.5.cloned.1.call-update) | async-done | bytes 1769488 | tf_op jit(solution)/shard_map/all_gather | solution.py:70
  237.8 3.7 fusion.21
  241.5 2.4 multiply_reduce_fusion.1
  244.0 2.0 fusion.47
  250.6 3.5 fusion.65
  254.1 152.4 %reduce-scatter.7.cloned.1.call-done = f32[72,24]{0,1:T(8,128)} async-done(((f32[72,1152]{0,1:T(8,128)}), f32[72,24]{0,1:T(8,128)}) %reduce-scatter.7.cloned.1.call-update) | async-done | bytes 6928
  406.6 178.9 %reduce-scatter.5.cloned.1.call-done = f32[24,216]{1,0:T(8,128)} async-done(((f32[1152,216]{1,0:T(8,128)}), f32[24,216]{1,0:T(8,128)}) %reduce-scatter.5.cloned.1.call-update) | async-done | bytes 20752 | tf_op jit(solution)/shard_map/reduce_scatter | solution.py:104
  (50 shorter events, 9.6 us)
Async XLA Ops:
  7.2 106.3 %copy-start = (bf16[1152,216]{0,1:T(8,128)(2,1)S(1)}, bf16[1152,216]{0,1:T(8,128)(2,1)}, u32[]{:S(2)}) copy-start(bf16[1152,216]{0,1:T(8,128)(2,1)} %param.8) | copy-start | bytes 1492996
  7.2 97.0 %all-gather.3.cloned.1.call-start = ((), (), s32[]{:S(2)}) async-start(), calls=%async_computation.2 | async-start | bytes 5013504 | tf_op jit(solution)/shard_map/all_gather | solution.py:26
  9.2 228.6 %all-gather.5.cloned.1.call-start = ((), (), s32[]{:S(2)}) async-start(), calls=%async_computation.3 | async-start | bytes 1806336 | tf_op jit(solution)/shard_map/all_gather | solution.py:70
  10.8 395.8 %reduce-scatter.7.cloned.1.call-start = ((), (), s32[]{:S(2)}) async-start(), calls=%async_computation.5 | async-start | bytes 602112
  112.0 1.4 copy-start.1
  121.8 6.1 %copy-start.4 = (bf16[72,1152]{1,0:T(8,128)(2,1)S(1)}, bf16[72,1152]{1,0:T(8,128)(2,1)}, u32[]{:S(2)}) copy-start(bf16[72,1152]{1,0:T(8,128)(2,1)} %param.9) | copy-start | bytes 497668
  127.8 65.4 %copy-start.7 = (f32[16]{0:T(128)S(1)}, f32[16]{0:T(128)}, u32[]{:S(2)}) copy-start(f32[16]{0:T(128)} %convert_divide_fusion) | copy-start | bytes 196
  127.8 110.0 %copy-start.9 = (s32[16]{0:T(128)S(1)}, s32[16]{0:T(128)}, u32[]{:S(2)}) copy-start(s32[16]{0:T(128)} %iota_add_fusion) | copy-start | bytes 196
  193.3 50.7 %copy-start.6 = (f32[16,1,72]{2,1,0:T(1,128)S(1)}, f32[16,1,72]{2,1,0:T(1,128)}, u32[]{:S(2)}) copy-start(f32[16,1,72]{2,1,0:T(1,128)} %fusion.12) | copy-start | bytes 13828
  237.8 8.5 %copy-start.5 = (bf16[16,64,1,1,72]{4,1,0,3,2:T(8,128)(2,1)S(1)}, bf16[16,64,1,1,72]{4,1,0,3,2:T(8,128)(2,1)}, u32[]{:S(2)}) copy-start(bf16[16,64,1,1,72]{4,1,0,3,2:T(8,128)(2,1)} %copy.41) | copy-start | bytes 442372
  237.8 8.5 %copy-start.8 = (f32[16,64]{1,0:T(8,128)S(1)}, f32[16,64]{1,0:T(8,128)}, u32[]{:S(2)}) copy-start(f32[16,64]{1,0:T(8,128)} %get-tuple-element.7) | copy-start | bytes 12292
  237.8 8.5 %copy-start.10 = (f32[16,64,64]{1,2,0:T(8,128)S(1)}, f32[16,64,64]{1,2,0:T(8,128)}, u32[]{:S(2)}) copy-start(f32[16,64,64]{1,2,0:T(8,128)} %get-tuple-element.13) | copy-start | bytes 786436
  237.8 8.5 %copy-start.11 = (f32[16,64]{1,0:T(8,128)S(1)}, f32[16,64]{1,0:T(8,128)}, u32[]{:S(2)}) copy-start(f32[16,64]{1,0:T(8,128)} %get-tuple-element.12) | copy-start | bytes 12292
  241.5 5.5 copy-start.2
  246.3 1.3 copy-start.3
  248.1 337.4 %reduce-scatter.5.cloned.1.call-start = ((), (), s32[]{:S(2)}) async-start(), calls=%async_computation.4 | async-start | bytes 1204224 | tf_op jit(solution)/shard_map/reduce_scatter | solution.py:104
Sparse Core Ops, SparseCore 0:
  10.4 93.7 all-gather.2
  107.9 129.8 all-gather.4
  248.2 158.3 reduce-scatter.6
  412.3 173.1 reduce-scatter.4
where the time goes:
time: 600 us; the launch traced here: 592 us
  waiting for transfers between devices  464 us (77%)
  blocking collectives  64 us (11%)
  matrix products  20.3 us (3%)
  local copies, waits for them, and re-layouts  19.5 us (3%)
  between operations  14.7 us (2%)
  other arithmetic  9.2 us (2%)
    reduce_scatter x1, waiting for transfers between devices, on_device(): lax.psum_scatter(grad_in, 'dp', scatter_dimension=0, tiled=True)  179 us
    unnamed x5, waiting for transfers between devices  153 us
    all_gather x1, waiting for transfers between devices, on_device(): gathered = lax.all_gather(hidden, 'mp', axis=2, tiled=True)  88.3 us
    psum x1, blocking collectives, on_device(): lax.psum(attn_term.astype(jnp.bfloat16), 'mp').astype(jnp.float32)  64 us
    all_gather x1, waiting for transfers between devices, on_device(): lax.all_gather(images.astype(jnp.bfloat16), 'dp', axis=0, tiled=True)  44.3 us
  transfers between devices with their start and end apart: 4, of which 4 were waited for; matrix products, arithmetic and copies ran while one was open for 6% of the time, Pallas kernels for 0%

commit v1 on v0

v1 whole, which is shorter than its diff:
```python
import jax
import jax.numpy as jnp
from jax import lax
from jax.experimental import pallas as pl
from jax.experimental.pallas import tpu as pltpu
from jax.sharding import PartitionSpec as P

D = 1152
HD = 72
L = 64
CAPS = 16
XN = 4
YN = 4
MP = XN * YN
SUB = 256
SUBS = CAPS * L // SUB
WIDE = 384
GO_AT = 256
OWN = 24
SLICES = D // 128

MESH = pl.DeviceIdType.MESH
F32 = jnp.float32
BF16 = jnp.bfloat16


def dot_nn(a, b):
    return lax.dot_general(a, b, (((1,), (0,)), ((), ())), preferred_element_type=F32)


def dot_nt(a, b):
    return lax.dot_general(a, b, (((1,), (1,)), ((), ())), preferred_element_type=F32)


def dot_tn(a, b):
    return lax.dot_general(a, b, (((0,), (0,)), ((), ())), preferred_element_type=F32)


def eye(n):
    rows = lax.broadcasted_iota(jnp.int32, (n, n), 0)
    cols = lax.broadcasted_iota(jnp.int32, (n, n), 1)
    return (rows == cols).astype(F32).astype(BF16)


def split_two(a):
    high = a.astype(BF16)
    return high, (a - high.astype(F32)).astype(BF16)


def make_kernel(zn):
    right_steps, left_steps = zn // 2, (zn - 1) // 2

    def kernel(
        hid, counts, w_qkv, w_out, images, params,
        gq_out, go_out,
        gat, nrm, wt, img, qt, kt, vt, vtok, prob, wl, live_sc,
        part, part_in, pooled_in, grad, sib_out, sib_in, z_out, z_in, acc, y_in,
        y_s, y_r, xr_s, xr_r, xl_s, xl_r, fr_s, fr_r, fl_s, fl_r,
        iy_s, iy_r, ir_s, ir_r, il_s, il_r, is_s, is_r,
        b1_s, b1_r, b2_s, b2_r, c1_s, c1_r, c2_s, c2_r, c3_s, c3_r,
    ):
        dp, mp = lax.axis_index("dp"), lax.axis_index("mp")
        core, yh, z = dp % 2, (dp // 2) % 2, dp // 4
        x, y = mp % XN, mp // XN
        sibling = (dp + 1 - 2 * core, mp)
        across = (dp + 2 - 4 * yh, mp)

        def at_z(step):
            return (z + zn + step) % zn

        def dev_z(step):
            return (at_z(step) * 4 + yh * 2 + core, mp)

        def slot(dx, dy):
            return ((y + YN + dy) % YN) * XN + (x + XN + dx) % XN

        def remote(src, dst, send, recv, device):
            return pltpu.make_async_remote_copy(
                src_ref=src, dst_ref=dst, send_sem=send, recv_sem=recv,
                device_id=device, device_id_type=MESH,
            )

        barrier = pltpu.get_barrier_semaphore()
        for step in range(1, MP):
            pl.semaphore_signal(barrier, inc=1, device_id=(dp, (mp + step) % MP), device_id_type=MESH)
        for step in range(1, zn):
            pl.semaphore_signal(barrier, inc=1, device_id=dev_z(step), device_id_type=MESH)
        pl.semaphore_signal(barrier, inc=1, device_id=sibling, device_id_type=MESH)
        pl.semaphore_signal(barrier, inc=1, device_id=across, device_id_type=MESH)

        eye_hd = eye(HD)
        for i in range(SUBS):
            gat[i // 2, mp, i % 2] = dot_nt(eye_hd, hid[i * SUB:(i + 1) * SUB, :]).astype(BF16)
        img[z, core, yh] = images[...].astype(BF16)

        pl.semaphore_wait(barrier, MP - 1 + zn - 1 + 2)

        def send_y(h, k):
            own = gat.at[h, mp]
            return remote(own, own, y_s.at[h, k - 1], y_r.at[h, k - 1], (dp, slot(0, k)))

        def recv_y(h, k):
            got = gat.at[h, slot(0, -k)]
            return remote(got, got, y_s.at[h, k - 1], y_r.at[h, k - 1], (dp, slot(0, k)))

        def send_xr(h, k):
            block = gat.at[h, slot(0, -k)]
            return remote(block, block, xr_s.at[h, k], xr_r.at[h, k], (dp, slot(1, 0)))

        def recv_xr(h, k):
            block = gat.at[h, slot(-1, -k)]
            return remote(block, block, xr_s.at[h, k], xr_r.at[h, k], (dp, slot(1, 0)))

        def send_xl(h, k):
            block = gat.at[h, slot(0, -k)]
            return remote(block, block, xl_s.at[h, k], xl_r.at[h, k], (dp, slot(-1, 0)))

        def recv_xl(h, k):
            block = gat.at[h, slot(1, -k)]
            return remote(block, block, xl_s.at[h, k], xl_r.at[h, k], (dp, slot(-1, 0)))

        def send_fr(h, k):
            block = gat.at[h, slot(-1, -k), 0]
            return remote(block, block, fr_s.at[h, k], fr_r.at[h, k], (dp, slot(1, 0)))

        def recv_fr(h, k):
            block = gat.at[h, slot(-2, -k), 0]
            return remote(block, block, fr_s.at[h, k], fr_r.at[h, k], (dp, slot(1, 0)))

        def send_fl(h, k):
            block = gat.at[h, slot(1, -k), 1]
            return remote(block, block, fl_s.at[h, k], fl_r.at[h, k], (dp, slot(-1, 0)))

        def recv_fl(h, k):
            block = gat.at[h, slot(2, -k), 1]
            return remote(block, block, fl_s.at[h, k], fl_r.at[h, k], (dp, slot(-1, 0)))

        def send_iy():
            own = img.at[z, core, yh]
            return remote(own, own, iy_s, iy_r, across)

        def recv_iy():
            got = img.at[z, core, 1 - yh]
            return remote(got, got, iy_s, iy_r, across)

        def send_ir(s):
            block = img.at[at_z(1 - s), core]
            return remote(block, block, ir_s.at[s - 1], ir_r.at[s - 1], dev_z(1))

        def recv_ir(s):
            block = img.at[at_z(-s), core]
            return remote(block, block, ir_s.at[s - 1], ir_r.at[s - 1], dev_z(1))

        def send_il(s):
            block = img.at[at_z(s - 1), core]
            return remote(block, block, il_s.at[s - 1], il_r.at[s - 1], dev_z(-1))

        def recv_il(s):
            block = img.at[at_z(s), core]
            return remote(block, block, il_s.at[s - 1], il_r.at[s - 1], dev_z(-1))

        def send_is(s):
            block = img.at[at_z(s), core]
            return remote(block, block, is_s.at[(s + zn) % zn], is_r.at[(s + zn) % zn], sibling)

        def recv_is(s):
            block = img.at[at_z(s), 1 - core]
            return remote(block, block, is_s.at[(s + zn) % zn], is_r.at[(s + zn) % zn], sibling)

        def image_step(s):
            if s == 1:
                recv_iy().wait_recv()
                send_is(0).start()
            elif s <= right_steps + 1:
                recv_ir(s - 1).wait_recv()
                if s - 1 <= left_steps:
                    recv_il(s - 1).wait_recv()
            if s <= right_steps:
                send_ir(s).start()
            if s <= left_steps:
                send_il(s).start()
            if s > 1:
                send_is(1 - s).start()
                if s - 1 <= left_steps:
                    send_is(s - 1).start()

        count_col = jnp.zeros((CAPS, 1), jnp.int32)
        row16 = lax.broadcasted_iota(jnp.int32, (CAPS, 1), 0)
        for c in range(CAPS):
            count_col = jnp.where(row16 == c, counts[c], count_col)
        inv_count = 1.0 / count_col.astype(F32)
        scale_inv = 1.0 / (float(HD) ** 0.5)

        for k in range(1, YN):
            send_y(0, k).start()
        send_xr(0, 0).start()
        send_xl(0, 0).start()
        send_iy().start()
        for k in range(1, YN):
            send_y(1, k).start()
        grad[...] = jnp.zeros_like(grad)
        eye_w = eye(3 * HD)
        for k in range(1, YN):
            recv_y(0, k).wait_recv()
            send_xr(0, k).start()
            send_xl(0, k).start()
        image_step(1)
        send_xr(1, 0).start()
        send_xl(1, 0).start()
        wt[...] = dot_nt(eye_w, w_qkv[...]).astype(BF16)
        for i in range(SUBS):
            caption = lax.broadcasted_iota(jnp.int32, (CAPS, SUB), 0)
            token = lax.broadcasted_iota(jnp.int32, (CAPS, SUB), 1) + (i * SUB)
            held = (token // L == caption) & (token % L < count_col)
            live_sc[i] = held.astype(F32)

        def forward_sub(h, s):
            i = h * 2 + s
            values = gat[h, :, s].astype(F32).reshape(D, SUB)
            center = jnp.sum(values, axis=0, keepdims=True) * (1.0 / D)
            values = values - center
            spread = jnp.sum(values * values, axis=0, keepdims=True) * (1.0 / D)
            normed = (values * lax.rsqrt(spread + 1e-06)).astype(BF16)
            nrm[i] = normed
            packed = dot_nn(wt[...], normed)
            q = packed[0:HD].astype(BF16)
            key = packed[HD:2 * HD].astype(BF16)
            val = packed[2 * HD:3 * HD].astype(BF16)
            qt[i] = q
            kt[i] = key
            vt[i] = val
            eye_s = eye(SUB)
            key_tok = dot_nt(eye_s, key).astype(BF16)
            vtok[i] = dot_nt(eye_s, val).astype(BF16)
            live_here = live_sc[i].astype(BF16)
            for b in range(SUB // 128):
                lanes = slice(b * 128, (b + 1) * 128)
                scores = dot_nn(key_tok[lanes], q[:, lanes]) * scale_inv
                first = (i * SUB + b * 128) // L
                s_row = lax.broadcasted_iota(jnp.int32, (128, 128), 0)
                t_col = lax.broadcasted_iota(jnp.int32, (128, 128), 1)
                limit = jnp.where(s_row < L, counts[first], counts[first + 1] + L)
                held = (s_row < limit) & (s_row // L == t_col // L)
                top = jnp.max(jnp.where(held, scores, -1e30), axis=0, keepdims=True)
                expo = jnp.where(held, jnp.exp(jnp.where(held, scores - top, 0.0)), 0.0)
                probs = expo / jnp.sum(expo, axis=0, keepdims=True)
                prob[i, b] = probs
                wl[i, :, lanes] = dot_nt(live_here[:, lanes], probs.astype(BF16))

        step = 2
        for k in range(YN):
            recv_xr(0, k).wait_recv()
            send_fr(0, k).start()
            recv_xl(0, k).wait_recv()
            send_fl(0, k).start()
            if k % 2 == 1:
                image_step(step)
                step += 1
        for k in range(1, YN):
            recv_y(1, k).wait_recv()
            send_xr(1, k).start()
            send_xl(1, k).start()
        for k in range(YN):
            recv_fr(0, k).wait_recv()
            recv_fl(0, k).wait_recv()
        if step <= right_steps + 1:
            image_step(step)
            step += 1
        forward_sub(0, 0)
        if step <= right_steps + 1:
            image_step(step)
            step += 1
        forward_sub(0, 1)
        for k in range(YN):
            recv_xr(1, k).wait_recv()
            send_fr(1, k).start()
            recv_xl(1, k).wait_recv()
            send_fl(1, k).start()
        while step <= right_steps + 1:
            image_step(step)
            step += 1
        for k in range(YN):
            recv_fr(1, k).wait_recv()
            recv_fl(1, k).wait_recv()
        forward_sub(1, 0)
        forward_sub(1, 1)

        mix = jnp.zeros((CAPS, HD), F32)
        hid_sum = jnp.zeros((CAPS, HD), F32)
        for i in range(SUBS):
            mix = mix + dot_nt(wl[i].astype(BF16), vt[i])
            hid_sum = hid_sum + dot_nn(live_sc[i].astype(BF16), hid[i * SUB:(i + 1) * SUB, :])
        mix = mix * inv_count
        hid_sum = hid_sum * inv_count
        place = (
            lax.broadcasted_iota(jnp.int32, (HD, D), 1)
            == lax.broadcasted_iota(jnp.int32, (HD, D), 0) + mp * HD
        ).astype(F32).astype(BF16)
        mix_hi, mix_lo = split_two(mix)
        hid_hi, hid_lo = split_two(hid_sum)
        w_rows = w_out[...]
        share = dot_nn(mix_hi, w_rows) + dot_nn(mix_lo, w_rows) + dot_nn(hid_hi, place) + dot_nn(hid_lo, place)
        for j in range(SLICES):
            part[j] = share[:, j * 128:(j + 1) * 128]

        def send_b1(j):
            return remote(part.at[j], part_in.at[mp], b1_s.at[j], b1_r.at[mp], (dp, j))

        def recv_b1(step):
            src = (mp + step) % MP
            return remote(part_in.at[src], part_in.at[src], b1_s.at[0], b1_r.at[src], (dp, mp))

        def send_b2(step):
            own = pooled_in.at[mp]
            return remote(own, own, b2_s.at[step - 1], b2_r.at[mp], (dp, (mp + step) % MP))

        def recv_b2(j):
            return remote(pooled_in.at[j], pooled_in.at[j], b2_s.at[0], b2_r.at[j], (dp, mp))

        for j in range(SLICES):
            @pl.when(mp != j)
            def _():
                send_b1(j).start()

        @pl.when(mp < SLICES)
        def _():
            total = part[mp]
            for step in range(1, MP):
                recv_b1(step).wait_recv()
                total = total + part_in[(mp + step) % MP]
            pooled_in[mp] = total
            for step in range(1, MP):
                send_b2(step).start()

        for s in range(1, zn):
            recv_is(s).wait_recv()
        recv_is(0).wait_recv()

        for j in range(SLICES):
            @pl.when(mp != j)
            def _():
                recv_b2(j).wait_recv()

        pooled = jnp.concatenate([pooled_in[j] for j in range(SLICES)], axis=1)
        inv_norm = lax.rsqrt(jnp.sum(pooled * pooled, axis=1, keepdims=True) + 1e-06)
        text_emb = pooled * inv_norm
        pictures = img[...].reshape(zn * 4 * CAPS, D)
        logit_scale = jnp.exp(jnp.full((CAPS, 1), params[0], F32))
        logits = logit_scale * dot_nt(text_emb.astype(BF16), pictures) + params[1]
        mine = ((z * 2 + core) * 2 + yh) * CAPS
        shape = (CAPS, zn * 4 * CAPS)
        same = lax.broadcasted_iota(jnp.int32, shape, 1) == lax.broadcasted_iota(jnp.int32, shape, 0) + mine
        label = jnp.where(same, 1.0, -1.0).astype(F32)
        pair_grad = -label * jax.nn.sigmoid(-label * logits)
        text_grad = logit_scale * dot_nn(pair_grad.astype(BF16), pictures)
        along = jnp.sum(text_emb * text_grad, axis=1, keepdims=True)
        pooled_grad = (text_grad - text_emb * along) * inv_norm
        grad[:, GO_AT:GO_AT + HD] = dot_tn(pooled_grad.astype(BF16), mix.astype(BF16))
        per_caption = dot_nt(w_rows, (pooled_grad * inv_count).astype(BF16)).astype(BF16)

        total = None
        for i in range(SUBS):
            pull = dot_nn(vtok[i], per_caption)
            owner = lax.broadcasted_iota(jnp.int32, (SUB, CAPS), 0) // L + (i * SUB // L)
            pull = jnp.sum(
                jnp.where(owner == lax.broadcasted_iota(jnp.int32, (SUB, CAPS), 1), pull, 0.0),
                axis=1, keepdims=True,
            )
            dq, dk = [], []
            for b in range(SUB // 128):
                lanes = slice(b * 128, (b + 1) * 128)
                first = (i * SUB + b * 128) // L
                t_row = lax.broadcasted_iota(jnp.int32, (1, 128), 1)
                limit = jnp.where(t_row < L, counts[first], counts[first + 1] + L)
                factor = jnp.where(t_row < limit, scale_inv, 0.0)
                probs = prob[i, b]
                here = pull[lanes]
                mean_pull = jnp.sum(probs * here, axis=0, keepdims=True)
                score_grad = (probs * (here - mean_pull) * factor).astype(BF16)
                dq.append(dot_nn(kt[i, :, lanes], score_grad))
                dk.append(dot_nt(qt[i, :, lanes], score_grad))
            dv = dot_nn(per_caption, wl[i].astype(BF16))
            qkv_grad = jnp.concatenate(
                [jnp.concatenate(dq, axis=1), jnp.concatenate(dk, axis=1), dv], axis=0
            ).astype(BF16)
            term = dot_nt(nrm[i], qkv_grad)
            total = term if total is None else total + term
        grad[:, 0:3 * HD] = total

        def hop(p):
            return (zn // 2 + ((p + 1) // 2) * (1 - 2 * (p % 2)) + zn) % zn

        def rows_of(step, which, half):
            first = at_z(step) * (4 * OWN) + half * (2 * OWN) + which * OWN
            return grad[pl.ds(pl.multiple_of(first, 8), OWN), :]

        def both(step, which):
            return jnp.concatenate([rows_of(step, which, 0), rows_of(step, which, 1)], axis=0)

        groups = 3
        per = zn // groups

        def send_c1(g):
            return remote(
                sib_out.at[pl.ds(g * per, per)], sib_in.at[pl.ds(g * per, per)],
                c1_s.at[g], c1_r.at[g], sibling,
            )

        def send_c2(p):
            return remote(z_out.at[p], z_in.at[p], c2_s.at[p], c2_r.at[p], dev_z(hop(p)))

        for g in range(groups):
            for p in range(g * per, (g + 1) * per):
                sib_out[p] = both(hop(p), 1 - core).astype(BF16)
            send_c1(g).start()
        for g in range(groups):
            send_c1(g).wait_recv()
            for p in range(g * per, (g + 1) * per):
                summed = both(hop(p), core) + sib_in[p].astype(F32)
                if p < zn - 1:
                    z_out[p] = summed.astype(BF16)
                    send_c2(p).start()
                else:
                    acc[...] = summed
        total = acc[...]
        for p in range(zn - 2, -1, -1):
            send_c2(p).wait_recv()
            total = total + z_in[p].astype(F32)
        acc[...] = total

        away = acc.at[pl.ds(pl.multiple_of((1 - yh) * OWN, 8), OWN)]
        last = remote(away, y_in, c3_s, c3_r, across)
        last.start()
        last.wait_recv()
        final = acc[pl.ds(pl.multiple_of(yh * OWN, 8), OWN), :] + y_in[...]
        gq_out[...] = final[:, 0:3 * HD]
        go_out[...] = final[:, GO_AT:GO_AT + HD]

        for h in range(2):
            for k in range(1, YN):
                send_y(h, k).wait_send()
            for k in range(YN):
                send_xr(h, k).wait_send()
                send_xl(h, k).wait_send()
                send_fr(h, k).wait_send()
                send_fl(h, k).wait_send()
        send_iy().wait_send()
        for s in range(1, right_steps + 1):
            send_ir(s).wait_send()
        for s in range(1, left_steps + 1):
            send_il(s).wait_send()
        for s in range(zn):
            send_is(s).wait_send()
        for j in range(SLICES):
            @pl.when(mp != j)
            def _():
                send_b1(j).wait_send()

        @pl.when(mp < SLICES)
        def _():
            for step in range(1, MP):
                send_b2(step).wait_send()

        for g in range(groups):
            send_c1(g).wait_send()
        for p in range(zn - 1):
            send_c2(p).wait_send()
        last.wait_send()

    return kernel


def solution(mesh):
    zn = mesh.shape["dp"] // 4
    dma = pltpu.SemaphoreType.DMA
    right_steps, left_steps = zn // 2, (zn - 1) // 2
    vmem = pl.BlockSpec(memory_space=pltpu.VMEM)
    smem = pl.BlockSpec(memory_space=pltpu.SMEM)

    def on_device(hidden, counts, w_qkv, w_out, images, logit_params):
        gq, go = pl.pallas_call(
            make_kernel(zn),
            out_shape=(
                jax.ShapeDtypeStruct((OWN, 3 * HD), F32),
                jax.ShapeDtypeStruct((OWN, HD), F32),
            ),
            in_specs=[vmem, smem, vmem, vmem, vmem, smem],
            out_specs=(vmem, vmem),
            scratch_shapes=[
                pltpu.VMEM((2, MP, 2, HD, SUB), BF16),
                pltpu.VMEM((SUBS, D, SUB), BF16),
                pltpu.VMEM((3 * HD, D), BF16),
                pltpu.VMEM((zn, 2, 2, CAPS, D), BF16),
                pltpu.VMEM((SUBS, HD, SUB), BF16),
                pltpu.VMEM((SUBS, HD, SUB), BF16),
                pltpu.VMEM((SUBS, HD, SUB), BF16),
                pltpu.VMEM((SUBS, SUB, HD), BF16),
                pltpu.VMEM((SUBS, SUB // 128, 128, 128), F32),
                pltpu.VMEM((SUBS, CAPS, SUB), F32),
                pltpu.VMEM((SUBS, CAPS, SUB), F32),
                pltpu.VMEM((SLICES, CAPS, 128), F32),
                pltpu.VMEM((MP, CAPS, 128), F32),
                pltpu.VMEM((SLICES, CAPS, 128), F32),
                pltpu.VMEM((D, WIDE), F32),
                pltpu.VMEM((zn, 2 * OWN, WIDE), BF16),
                pltpu.VMEM((zn, 2 * OWN, WIDE), BF16),
                pltpu.VMEM((zn - 1, 2 * OWN, WIDE), BF16),
                pltpu.VMEM((zn - 1, 2 * OWN, WIDE), BF16),
                pltpu.VMEM((2 * OWN, WIDE), F32),
                pltpu.VMEM((OWN, WIDE), F32),
                dma((2, YN - 1)), dma((2, YN - 1)),
                dma((2, YN)), dma((2, YN)), dma((2, YN)), dma((2, YN)),
                dma((2, YN)), dma((2, YN)), dma((2, YN)), dma((2, YN)),
                dma, dma,
                dma((right_steps,)), dma((right_steps,)), dma((left_steps,)), dma((left_steps,)),
                dma((zn,)), dma((zn,)),
                dma((SLICES,)), dma((MP,)), dma((MP - 1,)), dma((SLICES,)),
                dma((3,)), dma((3,)), dma((zn - 1,)), dma((zn - 1,)), dma, dma,
            ],
            compiler_params=pltpu.CompilerParams(
                collective_id=0, has_side_effects=True, vmem_limit_bytes=40 * 1024 * 1024
            ),
        )(hidden.reshape(CAPS * L, HD), counts, w_qkv, w_out, images, logit_params)
        return gq, go.T

    placed = (P("dp", None, "mp"), P("dp"), P(None, "mp"), P("mp", None), P("dp", None), P())
    return jax.shard_map(
        on_device,
        mesh=mesh,
        in_specs=placed,
        out_specs=(P("dp", "mp"), P("mp", "dp")),
        check_vma=False,
    )
```

time: 600 us -> 99.2 us (0.17); the launches traced: 592 us -> 99 us
  waiting for transfers between devices: 464 us -> 0 us
  Pallas kernels: 0 us -> 95.7 us
  blocking collectives: 64 us -> 0 us
  matrix products: 20.3 us -> 0 us
  local copies, waits for them, and re-layouts: 19.5 us -> 2.55 us
  between operations: 14.7 us -> 0.72 us
  other arithmetic: 9.2 us -> 0 us
    reduce_scatter x1 -> x0, waiting for transfers between devices: 179 us -> none  [on_device(): lax.psum_scatter(grad_in, 'dp', scatter_dimension=0, tiled=True)]
    unnamed x5 -> x0, waiting for transfers between devices: 153 us -> none
    all_gather x2 -> x0, waiting for transfers between devices: 133 us -> none  [the longest x1 88.3 us: on_device(): gathered = lax.all_gather(hidden, 'mp', axis=2, tiled=True)]
    pallas_call x0 -> x1, Pallas kernels: none -> 95.7 us  [on_device(): pl.pallas_call(make_kernel(zn), out_shape=(jax.ShapeDtypeStruct((OWN, 3 *...]
    psum x1 -> x0, blocking collectives: 64 us -> none  [on_device(): lax.psum(attn_term.astype(jnp.bfloat16), 'mp').astype(jnp.float32)]
    dot_general x14 -> x0, matrix products: 20.3 us -> none  [the longest x1 3.69 us: pair_terms(): jnp.dot(text_emb, incoming.T, precision=lax.Precision.HIGHEST)]
    all_gather x1 -> x0, local copies, waits for them, and re-layouts: 6.01 us -> none  [on_device(): gathered = lax.all_gather(hidden, 'mp', axis=2, tiled=True)]
  transfers between devices with their start and end apart: 4 -> 0, of which waited for: 4 -> 0; matrix products, arithmetic and copies ran while one was open for 6% -> 0% of each run, Pallas kernels for 0% -> 0%
where the time goes in v1:
time: 99.2 us; the launch traced here: 99 us
  Pallas kernels  95.7 us (96%)
  local copies, waits for them, and re-layouts  2.55 us (3%)
    pallas_call x1, Pallas kernels, on_device(): pl.pallas_call(make_kernel(zn), out_shape=(jax.ShapeDtypeStruct((OWN, 3 *...  95.7 us
    unnamed x13, local copies, waits for them, and re-layouts  2.55 us

profile of v1, /device:TPU:1, one launch (start us, length us, event | category | flops | bytes accessed | tf_op | source)
XLA Modules:
  0.0 99.0 jit_solution(2372232273312139012)
XLA Ops:
  0.6 0.0 copy-start
  0.6 0.0 copy-start.1
  0.7 0.0 copy-start.2
  0.7 0.0 copy-start.3
  0.7 0.0 copy-start.4
  0.7 1.3 %copy.8.w_qkv = bf16[1152,216]{1,0:T(8,128)(2,1)S(1)} copy(bf16[1152,216]{0,1:T(8,128)(2,1)} %param.8) | data formatting | bytes 995328 | tf_op args[2]
  2.0 0.0 copy-done
  2.0 0.0 copy-done.1
  2.0 0.0 copy-done.2
  2.0 0.0 copy-done.3
  2.0 0.0 copy-done.4
  2.1 95.7 %shard_map.77 = (f32[24,216]{1,0:T(8,128)S(1)}, f32[24,72]{1,0:T(8,128)S(1)}) custom-call(bf16[1024,72]{1,0:T(8,128)(2,1)S(1)} %bitcast.2, s32[16]{0:T(128)S(1)} %copy-done.3, bf16[1152,216]{1,0:T(8,128)(2,1)S(1)} %copy.8.w_qkv, bf16[72,1152]{1,0:T(8,128)(2,1)S(1)} %copy-done.1, f32[16,1152]{1,0:T(8,128)S(1)} %copy-done.2, f32[2]{0:T(128)S(1)} %copy-done.4), custom_call_target="tpu_custom_call" | custom-call | tf_op jit(solution)/shard_map/pallas_call | solution.py:481
  97.8 0.6 copy.11
  98.4 0.6 copy.12
Async XLA Ops:
  0.6 1.4 %copy-start = (bf16[16,64,72]{2,1,0:T(8,128)(2,1)S(1)}, bf16[16,64,72]{2,1,0:T(8,128)(2,1)}, u32[]{:S(2)}) copy-start(bf16[16,64,72]{2,1,0:T(8,128)(2,1)} %param.6) | copy-start | bytes 442372
  0.6 1.4 %copy-start.1 = (bf16[72,1152]{1,0:T(8,128)(2,1)S(1)}, bf16[72,1152]{1,0:T(8,128)(2,1)}, u32[]{:S(2)}) copy-start(bf16[72,1152]{1,0:T(8,128)(2,1)} %w_out.1) | copy-start | bytes 497668
  0.7 1.4 %copy-start.2 = (f32[16,1152]{1,0:T(8,128)S(1)}, f32[16,1152]{1,0:T(8,128)}, u32[]{:S(2)}) copy-start(f32[16,1152]{1,0:T(8,128)} %images.1) | copy-start | bytes 221188
  0.7 1.4 %copy-start.3 = (s32[16]{0:T(128)S(1)}, s32[16]{0:T(128)}, u32[]{:S(2)}) copy-start(s32[16]{0:T(128)} %counts.1) | copy-start | bytes 196
  0.7 1.4 %copy-start.4 = (f32[2]{0:T(128)S(1)}, f32[2]{0:T(128)}, u32[]{:S(2)}) copy-start(f32[2]{0:T(128)} %params.1) | copy-start | bytes 28

commit v2 on v1

v2 whole, which is shorter than its diff:
```python
import jax
import jax.numpy as jnp
from jax import lax
from jax.experimental import pallas as pl
from jax.experimental.pallas import tpu as pltpu
from jax.sharding import PartitionSpec as P

D = 1152
HD = 72
L = 64
CAPS = 16
XN = 4
YN = 4
MP = XN * YN
SUB = 256
SUBS = CAPS * L // SUB
WIDE = 256
OWN = 24
ROWS = 32
GROUPS = 3
SLICES = D // 128

MESH = pl.DeviceIdType.MESH
F32 = jnp.float32
BF16 = jnp.bfloat16


def dot_nn(a, b):
    return lax.dot_general(a, b, (((1,), (0,)), ((), ())), preferred_element_type=F32)


def dot_nt(a, b):
    return lax.dot_general(a, b, (((1,), (1,)), ((), ())), preferred_element_type=F32)


def dot_tn(a, b):
    return lax.dot_general(a, b, (((0,), (0,)), ((), ())), preferred_element_type=F32)


def eye(n):
    rows = lax.broadcasted_iota(jnp.int32, (n, n), 0)
    cols = lax.broadcasted_iota(jnp.int32, (n, n), 1)
    return (rows == cols).astype(F32).astype(BF16)


def split_two(a):
    high = a.astype(BF16)
    return high, (a - high.astype(F32)).astype(BF16)


def make_kernel(zn):
    right_most, left_most = zn // 2, (zn - 1) // 2
    dests = 2 * zn
    per = dests // GROUPS

    def kernel(
        hid, counts, wt, w_out, images, params,
        gq_out, go_out,
        gat, nrm, img, qt, kt, vt, vtok, prob, wl, live_sc, share_hid,
        part, part_in, pooled_in, grad, outer, sib_out, sib_in, z_out, z_in, acc,
        y_s, y_r, yf_s, xr_s, xr_r, xl_s, xl_r, fr_s, fr_r, fl_s, fl_r,
        iy_s, iy_r, ir_s, ir_r, il_s, il_r, is_s, is_r,
        b1_s, b1_r, b2_s, b2_r, c1_s, c1_r, c2_s, c2_r,
    ):
        dp, mp = lax.axis_index("dp"), lax.axis_index("mp")
        core, yh, z = dp % 2, (dp // 2) % 2, dp // 4
        x, y = mp % XN, mp // XN
        sibling = (dp + 1 - 2 * core, mp)
        across = (dp + 2 - 4 * yh, mp)

        def at_z(step):
            return (z + zn + step) % zn

        def dev_z(step):
            return (at_z(step) * 4 + yh * 2 + core, mp)

        def hop(p):
            q = p // 2
            return (zn // 2 + ((q + 1) // 2) * (1 - 2 * (q % 2)) + zn) % zn

        def side(p):
            return yh if p % 2 == 1 else 1 - yh

        def dev_c(p):
            return (at_z(hop(p)) * 4 + side(p) * 2 + core, mp)

        def slot(dx, dy):
            return ((y + YN + dy) % YN) * XN + (x + XN + dx) % XN

        def remote(src, dst, send, recv, device):
            return pltpu.make_async_remote_copy(
                src_ref=src, dst_ref=dst, send_sem=send, recv_sem=recv,
                device_id=device, device_id_type=MESH,
            )

        barrier = pltpu.get_barrier_semaphore()
        for step in range(1, MP):
            pl.semaphore_signal(barrier, inc=1, device_id=(dp, (mp + step) % MP), device_id_type=MESH)
        for p in range(dests - 1):
            pl.semaphore_signal(barrier, inc=1, device_id=dev_c(p), device_id_type=MESH)
        pl.semaphore_signal(barrier, inc=1, device_id=sibling, device_id_type=MESH)

        eye_hd = eye(HD)
        for i in range(SUBS):
            gat[i // 2, mp, i % 2] = dot_nt(eye_hd, hid[i * SUB:(i + 1) * SUB, :]).astype(BF16)
        img[z, core, yh] = images[...].astype(BF16)

        count_col = jnp.zeros((CAPS, 1), jnp.int32)
        row16 = lax.broadcasted_iota(jnp.int32, (CAPS, 1), 0)
        for c in range(CAPS):
            count_col = jnp.where(row16 == c, counts[c], count_col)
        inv_count = 1.0 / count_col.astype(F32)
        scale_inv = 1.0 / (float(HD) ** 0.5)
        for i in range(SUBS):
            caption = lax.broadcasted_iota(jnp.int32, (CAPS, SUB), 0)
            token = lax.broadcasted_iota(jnp.int32, (CAPS, SUB), 1) + (i * SUB)
            held = (token // L == caption) & (token % L < count_col)
            live_sc[i] = held.astype(F32)
        hid_sum = jnp.zeros((CAPS, HD), F32)
        for i in range(SUBS):
            hid_sum = hid_sum + dot_nn(live_sc[i].astype(BF16), hid[i * SUB:(i + 1) * SUB, :])
        hid_hi, hid_lo = split_two(hid_sum * inv_count)
        place = (
            lax.broadcasted_iota(jnp.int32, (HD, D), 1)
            == lax.broadcasted_iota(jnp.int32, (HD, D), 0) + mp * HD
        ).astype(F32).astype(BF16)
        share_hid[...] = dot_nn(hid_hi, place) + dot_nn(hid_lo, place)
        grad[...] = jnp.zeros_like(grad)
        outer[...] = jnp.zeros_like(outer)

        pl.semaphore_wait(barrier, MP - 1 + dests - 1 + 1)

        def send_y(h, k):
            own = gat.at[h, mp]
            return remote(own, own, y_s.at[h, k - 1], y_r.at[h, k - 1], (dp, slot(0, k)))

        def recv_y(h, k):
            got = gat.at[h, slot(0, -k)]
            return remote(got, got, y_s.at[h, k - 1], y_r.at[h, k - 1], (dp, slot(0, k)))

        def forward_y(h, up):
            block = gat.at[h, slot(0, -2)]
            if up:
                return remote(block, block, yf_s.at[h], y_r.at[h, 2], (dp, slot(0, 1)))
            return remote(block, block, yf_s.at[h], y_r.at[h, 0], (dp, slot(0, -1)))

        def each_y(h, act):
            @pl.when(y != 3)
            def _():
                act(send_y(h, 1))

            act(send_y(h, 2))

            @pl.when(y != 0)
            def _():
                act(send_y(h, 3))

        def each_forward_y(h, act):
            @pl.when(y == 1)
            def _():
                act(forward_y(h, False))

            @pl.when(y == 2)
            def _():
                act(forward_y(h, True))

        k_near = 3 - 2 * (y % 2)
        k_far = 1 + (y + 1) // 2
        order = (0, k_near, 6 - k_near - k_far, k_far)

        def send_xr(h, k):
            block = gat.at[h, slot(0, -k)]
            return remote(block, block, xr_s.at[h, k], xr_r.at[h, k], (dp, slot(1, 0)))

        def recv_xr(h, k):
            block = gat.at[h, slot(-1, -k)]
            return remote(block, block, xr_s.at[h, k], xr_r.at[h, k], (dp, slot(1, 0)))

        def send_xl(h, k):
            block = gat.at[h, slot(0, -k)]
            return remote(block, block, xl_s.at[h, k], xl_r.at[h, k], (dp, slot(-1, 0)))

        def recv_xl(h, k):
            block = gat.at[h, slot(1, -k)]
            return remote(block, block, xl_s.at[h, k], xl_r.at[h, k], (dp, slot(-1, 0)))

        def send_fr(h, k):
            block = gat.at[h, slot(-1, -k), 0]
            return remote(block, block, fr_s.at[h, k], fr_r.at[h, k], (dp, slot(1, 0)))

        def recv_fr(h, k):
            block = gat.at[h, slot(-2, -k), 0]
            return remote(block, block, fr_s.at[h, k], fr_r.at[h, k], (dp, slot(1, 0)))

        def send_fl(h, k):
            block = gat.at[h, slot(1, -k), 1]
            return remote(block, block, fl_s.at[h, k], fl_r.at[h, k], (dp, slot(-1, 0)))

        def recv_fl(h, k):
            block = gat.at[h, slot(2, -k), 1]
            return remote(block, block, fl_s.at[h, k], fl_r.at[h, k], (dp, slot(-1, 0)))

        def line(q):
            return yh if q == 0 else 1 - yh

        def send_iy():
            own = img.at[z, core, yh]
            return remote(own, own, iy_s, iy_r, across)

        def recv_iy():
            got = img.at[z, core, 1 - yh]
            return remote(got, got, iy_s, iy_r, across)

        def send_ir(q, d):
            reach = 2 - d % 2
            block = img.at[at_z(reach - d), core, line(q)]
            return remote(block, block, ir_s.at[q, d - 1], ir_r.at[q, d - 1], dev_z(reach))

        def recv_ir(q, d):
            block = img.at[at_z(-d), core, line(q)]
            return remote(block, block, ir_s.at[q, d - 1], ir_r.at[q, d - 1], dev_z(1))

        def send_il(q, d):
            reach = 2 - d % 2
            block = img.at[at_z(d - reach), core, line(q)]
            return remote(block, block, il_s.at[q, d - 1], il_r.at[q, d - 1], dev_z(-reach))

        def recv_il(q, d):
            block = img.at[at_z(d), core, line(q)]
            return remote(block, block, il_s.at[q, d - 1], il_r.at[q, d - 1], dev_z(-1))

        def send_is(q, s):
            block = img.at[at_z(s), core, line(q)]
            n = (s + zn) % zn
            return remote(block, block, is_s.at[q, n], is_r.at[q, n], sibling)

        def recv_is(q, s):
            block = img.at[at_z(s), 1 - core, line(q)]
            n = (s + zn) % zn
            return remote(block, block, is_s.at[q, n], is_r.at[q, n], sibling)

        def image_step(q, step):
            near, far = 2 * step - 3, 2 * step - 2
            if step == 1:
                if q == 1:
                    recv_iy().wait_recv()
            else:
                for d in (far, near):
                    if d <= right_most:
                        recv_ir(q, d).wait_recv()
                    if d <= left_most:
                        recv_il(q, d).wait_recv()
                    if d == far and d + 1 <= right_most:
                        send_ir(q, d + 1).start()
                        if d + 2 <= right_most:
                            send_ir(q, d + 2).start()
                    if d == far and d + 1 <= left_most:
                        send_il(q, d + 1).start()
                        if d + 2 <= left_most:
                            send_il(q, d + 2).start()
                    if d <= right_most:
                        send_is(q, -d).start()
                    if d <= left_most:
                        send_is(q, d).start()
            if step == 1:
                for d in (2, 1):
                    send_ir(q, d).start()
                    send_il(q, d).start()
                send_is(q, 0).start()

        last_step = (right_most + 1) // 2 + 1

        each_y(0, lambda c: c.start())
        send_xr(0, 0).start()
        send_xl(0, 0).start()
        send_iy().start()
        image_step(0, 1)
        send_xr(1, 0).start()
        send_xl(1, 0).start()
        each_y(1, lambda c: c.start())

        def y_to_x(h, n):
            k = order[n]
            recv_y(h, k).wait_recv()
            if n == 3:
                each_forward_y(h, lambda c: c.start())
            send_xr(h, k).start()
            send_xl(h, k).start()

        def pass_on(h, n):
            k = order[n]
            recv_xr(h, k).wait_recv()
            send_fr(h, k).start()
            recv_xl(h, k).wait_recv()
            send_fl(h, k).start()

        def all_in(h):
            for k in range(YN):
                recv_fr(h, k).wait_recv()
                recv_fl(h, k).wait_recv()

        def forward_sub(h, s):
            i = h * 2 + s
            values = gat[h, :, s].astype(F32).reshape(D, SUB)
            center = jnp.sum(values, axis=0, keepdims=True) * (1.0 / D)
            values = values - center
            spread = jnp.sum(values * values, axis=0, keepdims=True) * (1.0 / D)
            normed = (values * lax.rsqrt(spread + 1e-06)).astype(BF16)
            nrm[i] = normed
            packed = dot_nn(wt[...], normed)
            q = packed[0:HD].astype(BF16)
            key = packed[HD:2 * HD].astype(BF16)
            val = packed[2 * HD:3 * HD].astype(BF16)
            qt[i] = q
            kt[i] = key
            vt[i] = val
            eye_s = eye(SUB)
            key_tok = dot_nt(eye_s, key).astype(BF16)
            vtok[i] = dot_nt(eye_s, val).astype(BF16)
            live_here = live_sc[i].astype(BF16)
            for b in range(SUB // 128):
                lanes = slice(b * 128, (b + 1) * 128)
                scores = dot_nn(key_tok[lanes], q[:, lanes]) * scale_inv
                first = (i * SUB + b * 128) // L
                s_row = lax.broadcasted_iota(jnp.int32, (128, 128), 0)
                t_col = lax.broadcasted_iota(jnp.int32, (128, 128), 1)
                limit = jnp.where(s_row < L, counts[first], counts[first + 1] + L)
                held = (s_row < limit) & (s_row // L == t_col // L)
                top = jnp.max(jnp.where(held, scores, -1e30), axis=0, keepdims=True)
                expo = jnp.where(held, jnp.exp(jnp.where(held, scores - top, 0.0)), 0.0)
                probs = expo / jnp.sum(expo, axis=0, keepdims=True)
                prob[i, b] = probs
                wl[i, :, lanes] = dot_nt(live_here[:, lanes], probs.astype(BF16))

        for n in range(1, YN):
            y_to_x(0, n)
        pass_on(0, 0)
        image_step(0, 2)
        y_to_x(1, 1)
        pass_on(0, 1)
        image_step(1, 1)
        y_to_x(1, 2)
        pass_on(0, 2)
        y_to_x(1, 3)
        pass_on(0, 3)
        image_step(0, 3)
        pass_on(1, 0)
        image_step(1, 2)
        pass_on(1, 1)
        for step in range(4, last_step + 1):
            image_step(0, step)
        pass_on(1, 2)
        pass_on(1, 3)
        all_in(0)
        forward_sub(0, 0)
        image_step(1, 3)
        forward_sub(0, 1)
        all_in(1)
        forward_sub(1, 0)
        forward_sub(1, 1)

        mix = jnp.zeros((CAPS, HD), F32)
        for i in range(SUBS):
            mix = mix + dot_nt(wl[i].astype(BF16), vt[i])
        mix = mix * inv_count
        mix_hi, mix_lo = split_two(mix)
        w_rows = w_out[...]
        share = dot_nn(mix_hi, w_rows) + dot_nn(mix_lo, w_rows) + share_hid[...]
        for j in range(SLICES):
            part[j] = share[:, j * 128:(j + 1) * 128]

        def send_b1(j):
            return remote(part.at[j], part_in.at[mp], b1_s.at[j], b1_r.at[mp], (dp, j))

        def recv_b1(step):
            src = (mp + step) % MP
            return remote(part_in.at[src], part_in.at[src], b1_s.at[0], b1_r.at[src], (dp, mp))

        def send_b2(step):
            own = pooled_in.at[mp]
            return remote(own, own, b2_s.at[step - 1], b2_r.at[mp], (dp, (mp + step) % MP))

        def recv_b2(j):
            return remote(pooled_in.at[j], pooled_in.at[j], b2_s.at[0], b2_r.at[j], (dp, mp))

        for j in range(SLICES):
            @pl.when(mp != j)
            def _():
                send_b1(j).start()

        for step in range(4, last_step + 1):
            image_step(1, step)

        @pl.when(mp < SLICES)
        def _():
            total = part[mp]
            for step in range(1, MP):
                recv_b1(step).wait_recv()
                total = total + part_in[(mp + step) % MP]
            pooled_in[mp] = total
            for step in range(1, MP):
                send_b2(step).start()

        for q in range(2):
            for s in range(zn):
                recv_is(q, s).wait_recv()

        for j in range(SLICES):
            @pl.when(mp != j)
            def _():
                recv_b2(j).wait_recv()

        pooled = jnp.concatenate([pooled_in[j] for j in range(SLICES)], axis=1)
        inv_norm = lax.rsqrt(jnp.sum(pooled * pooled, axis=1, keepdims=True) + 1e-06)
        text_emb = pooled * inv_norm
        pictures = img[...].reshape(zn * 4 * CAPS, D)
        logit_scale = jnp.exp(jnp.full((CAPS, 1), params[0], F32))
        logits = logit_scale * dot_nt(text_emb.astype(BF16), pictures) + params[1]
        mine = ((z * 2 + core) * 2 + yh) * CAPS
        shape = (CAPS, zn * 4 * CAPS)
        same = lax.broadcasted_iota(jnp.int32, shape, 1) == lax.broadcasted_iota(jnp.int32, shape, 0) + mine
        label = jnp.where(same, 1.0, -1.0).astype(F32)
        pair_grad = -label * jax.nn.sigmoid(-label * logits)
        text_grad = logit_scale * dot_nn(pair_grad.astype(BF16), pictures)
        along = jnp.sum(text_emb * text_grad, axis=1, keepdims=True)
        pooled_grad = (text_grad - text_emb * along) * inv_norm
        lane = lax.broadcasted_iota(jnp.int32, (HD, 3 * HD), 1)
        tile = (lane % HD == lax.broadcasted_iota(jnp.int32, (HD, 3 * HD), 0)).astype(F32).astype(BF16)
        mix_tiled = dot_nn(mix_hi, tile)
        grad_cols = dot_tn(pooled_grad.astype(BF16), eye(CAPS)).reshape(D // OWN, 3, 8, CAPS)
        lane = lax.broadcasted_iota(jnp.int32, (CAPS, 3 * HD), 1)
        total = None
        for b in range(3):
            term = dot_nn(
                grad_cols[:, b].reshape(D // 3, CAPS).astype(BF16),
                jnp.where(lane // HD == b, mix_tiled, 0.0).astype(BF16),
            )
            total = term if total is None else total + term
        outer[:, 0:3 * HD] = total
        per_caption = dot_nt(w_rows, (pooled_grad * inv_count).astype(BF16)).astype(BF16)

        grads = []
        for i in range(SUBS):
            pull = dot_nn(vtok[i], per_caption)
            owner = lax.broadcasted_iota(jnp.int32, (SUB, CAPS), 0) // L + (i * SUB // L)
            pull = jnp.sum(
                jnp.where(owner == lax.broadcasted_iota(jnp.int32, (SUB, CAPS), 1), pull, 0.0),
                axis=1, keepdims=True,
            )
            dq, dk = [], []
            for b in range(SUB // 128):
                lanes = slice(b * 128, (b + 1) * 128)
                first = (i * SUB + b * 128) // L
                t_row = lax.broadcasted_iota(jnp.int32, (1, 128), 1)
                limit = jnp.where(t_row < L, counts[first], counts[first + 1] + L)
                factor = jnp.where(t_row < limit, scale_inv, 0.0)
                probs = prob[i, b]
                here = pull[lanes]
                mean_pull = jnp.sum(probs * here, axis=0, keepdims=True)
                score_grad = (probs * (here - mean_pull) * factor).astype(BF16)
                dq.append(dot_nn(kt[i, :, lanes], score_grad))
                dk.append(dot_nt(qt[i, :, lanes], score_grad))
            dv = dot_nn(per_caption, wl[i].astype(BF16))
            qkv_grad = jnp.concatenate(
                [jnp.concatenate(dq, axis=1), jnp.concatenate(dk, axis=1), dv], axis=0
            ).astype(BF16)
            grads.append(qkv_grad)

        chips = per // 2

        def first_row(p):
            return at_z(hop(p)) * 4 + side(p) * 2

        def rows_of(p, which):
            inside = (p // 2 % chips) * (4 * OWN) + side(p) * (2 * OWN) + which * OWN
            return jnp.concatenate(
                [
                    grad[p // per, pl.ds(pl.multiple_of(inside, 8), OWN), :],
                    outer[pl.ds(pl.multiple_of((first_row(p) + which) * 8, 8), 8), :],
                ],
                axis=0,
            )

        def send_c1(g):
            return remote(
                sib_out.at[pl.ds(g * per, per)], sib_in.at[pl.ds(g * per, per)],
                c1_s.at[g], c1_r.at[g], sibling,
            )

        def send_c2(p):
            return remote(z_out.at[p], z_in.at[p], c2_s.at[p], c2_r.at[p], dev_c(p))

        def group_grad(g):
            total = None
            for i in range(SUBS):
                left = jnp.concatenate(
                    [
                        nrm[i, pl.ds(pl.multiple_of(at_z(hop(p)) * (4 * OWN), 32), 4 * OWN), :]
                        for p in range(g * per, (g + 1) * per, 2)
                    ],
                    axis=0,
                )
                term = dot_nt(left, grads[i])
                total = term if total is None else total + term
            grad[g, :, 0:3 * HD] = total
            for p in range(g * per, (g + 1) * per):
                sib_out[p] = rows_of(p, 1 - core).astype(BF16)
            send_c1(g).start()

        def group_send(g):
            send_c1(g).wait_recv()
            for p in range(g * per, (g + 1) * per):
                summed = rows_of(p, core) + sib_in[p].astype(F32)
                if p < dests - 1:
                    z_out[p] = summed.astype(BF16)
                    send_c2(p).start()
                else:
                    acc[...] = summed

        group_grad(0)
        for g in range(1, GROUPS):
            group_grad(g)
            group_send(g - 1)
        group_send(GROUPS - 1)
        total = acc[...]
        for p in range(dests - 1):
            send_c2(p).wait_recv()
            total = total + z_in[p].astype(F32)
        gq_out[...] = total[0:OWN, 0:3 * HD]
        go_out[...] = jnp.concatenate(
            [total[OWN:ROWS, b * HD:(b + 1) * HD] for b in range(3)], axis=0
        )

        for h in range(2):
            each_y(h, lambda c: c.wait_send())
            each_forward_y(h, lambda c: c.wait_send())
            for k in range(YN):
                send_xr(h, k).wait_send()
                send_xl(h, k).wait_send()
                send_fr(h, k).wait_send()
                send_fl(h, k).wait_send()
        send_iy().wait_send()
        for q in range(2):
            for d in range(1, right_most + 1):
                send_ir(q, d).wait_send()
            for d in range(1, left_most + 1):
                send_il(q, d).wait_send()
            for s in range(zn):
                send_is(q, s).wait_send()
        for j in range(SLICES):
            @pl.when(mp != j)
            def _():
                send_b1(j).wait_send()

        @pl.when(mp < SLICES)
        def _():
            for step in range(1, MP):
                send_b2(step).wait_send()

        for g in range(GROUPS):
            send_c1(g).wait_send()
        for p in range(dests - 1):
            send_c2(p).wait_send()

    return kernel


def solution(mesh):
    zn = mesh.shape["dp"] // 4
    dma = pltpu.SemaphoreType.DMA
    right_most, left_most = zn // 2, (zn - 1) // 2
    dests = 2 * zn
    vmem = pl.BlockSpec(memory_space=pltpu.VMEM)
    smem = pl.BlockSpec(memory_space=pltpu.SMEM)

    def on_device(hidden, counts, w_qkv, w_out, images, logit_params):
        gq, go = pl.pallas_call(
            make_kernel(zn),
            out_shape=(
                jax.ShapeDtypeStruct((OWN, 3 * HD), F32),
                jax.ShapeDtypeStruct((OWN, HD), F32),
            ),
            in_specs=[vmem, smem, vmem, vmem, vmem, smem],
            out_specs=(vmem, vmem),
            scratch_shapes=[
                pltpu.VMEM((2, MP, 2, HD, SUB), BF16),
                pltpu.VMEM((SUBS, D, SUB), BF16),
                pltpu.VMEM((zn, 2, 2, CAPS, D), BF16),
                pltpu.VMEM((SUBS, HD, SUB), BF16),
                pltpu.VMEM((SUBS, HD, SUB), BF16),
                pltpu.VMEM((SUBS, HD, SUB), BF16),
                pltpu.VMEM((SUBS, SUB, HD), BF16),
                pltpu.VMEM((SUBS, SUB // 128, 128, 128), F32),
                pltpu.VMEM((SUBS, CAPS, SUB), F32),
                pltpu.VMEM((SUBS, CAPS, SUB), F32),
                pltpu.VMEM((CAPS, D), F32),
                pltpu.VMEM((SLICES, CAPS, 128), F32),
                pltpu.VMEM((MP, CAPS, 128), F32),
                pltpu.VMEM((SLICES, CAPS, 128), F32),
                pltpu.VMEM((GROUPS, D // GROUPS, WIDE), F32),
                pltpu.VMEM((D // 3, WIDE), F32),
                pltpu.VMEM((dests, ROWS, WIDE), BF16),
                pltpu.VMEM((dests, ROWS, WIDE), BF16),
                pltpu.VMEM((dests - 1, ROWS, WIDE), BF16),
                pltpu.VMEM((dests - 1, ROWS, WIDE), BF16),
                pltpu.VMEM((ROWS, WIDE), F32),
                dma((2, YN - 1)), dma((2, YN - 1)), dma((2,)),
                dma((2, YN)), dma((2, YN)), dma((2, YN)), dma((2, YN)),
                dma((2, YN)), dma((2, YN)), dma((2, YN)), dma((2, YN)),
                dma, dma,
                dma((2, right_most)), dma((2, right_most)), dma((2, left_most)), dma((2, left_most)),
                dma((2, zn)), dma((2, zn)),
                dma((SLICES,)), dma((MP,)), dma((MP - 1,)), dma((SLICES,)),
                dma((GROUPS,)), dma((GROUPS,)), dma((dests - 1,)), dma((dests - 1,)),
            ],
            compiler_params=pltpu.CompilerParams(
                collective_id=0, has_side_effects=True, vmem_limit_bytes=40 * 1024 * 1024
            ),
        )(hidden.reshape(CAPS * L, HD), counts, w_qkv.T, w_out, images, logit_params)
        return gq, go.T

    placed = (P("dp", None, "mp"), P("dp"), P(None, "mp"), P("mp", None), P("dp", None), P())
    return jax.shard_map(
        on_device,
        mesh=mesh,
        in_specs=placed,
        out_specs=(P("dp", "mp"), P("mp", "dp")),
        check_vma=False,
    )
```

time: 99.2 us -> 92.3 us (0.930)
  Pallas kernels: 95.7 us -> 85.7 us
  local copies, waits for them, and re-layouts: 2.55 us -> 5.65 us
    pallas_call x1, Pallas kernels: 95.7 us -> 85.7 us  [on_device(): pl.pallas_call(make_kernel(zn), out_shape=(jax.ShapeDtypeStruct((OWN, 3 *...]
    unnamed x13 -> x14, local copies, waits for them, and re-layouts: 2.55 us -> 5.65 us
where the time goes in v2:
time: 92.3 us; the launch traced here: 92 us
  Pallas kernels  85.7 us (93%)
  local copies, waits for them, and re-layouts  5.65 us (6%)
    pallas_call x1, Pallas kernels, on_device(): pl.pallas_call(make_kernel(zn), out_shape=(jax.ShapeDtypeStruct((OWN, 3 *...  85.7 us
    unnamed x14, local copies, waits for them, and re-layouts  5.65 us

profile of v2, /device:TPU:1, one launch (start us, length us, event | category | flops | bytes accessed | tf_op | source)
XLA Modules:
  0.0 92.0 jit_solution(17317686688427580334)
XLA Ops:
  0.6 0.0 copy-start.4
  0.6 0.0 copy-start.5
  0.7 0.6 copy-done.4
  1.3 0.0 copy-done.5
  1.3 0.0 copy-start
  1.3 1.0 %copy-done = bf16[1152,216]{0,1:T(8,128)(2,1)S(1)} copy-done((bf16[1152,216]{0,1:T(8,128)(2,1)S(1)}, bf16[1152,216]{0,1:T(8,128)(2,1)}, u32[]{:S(2)}) %copy-start) | copy-done | bytes 497688
  2.3 0.0 copy-start.1
  2.3 0.9 %copy-done.1 = bf16[16,64,72]{2,1,0:T(8,128)(2,1)S(1)} copy-done((bf16[16,64,72]{2,1,0:T(8,128)(2,1)S(1)}, bf16[16,64,72]{2,1,0:T(8,128)(2,1)}, u32[]{:S(2)}) %copy-start.1) | copy-done | bytes 147480
  3.3 0.0 copy-start.2
  3.3 0.9 copy-done.2
  4.2 0.0 copy-start.3
  4.2 0.9 copy-done.3
  5.1 85.7 %shard_map.77 = (f32[24,216]{1,0:T(8,128)S(1)}, f32[24,72]{1,0:T(8,128)S(1)}) custom-call(bf16[1024,72]{1,0:T(8,128)(2,1)S(1)} %bitcast.4, s32[16]{0:T(128)S(1)} %copy-done.4, bf16[216,1152]{1,0:T(8,128)(2,1)S(1)} %bitcast.3, bf16[72,1152]{1,0:T(8,128)(2,1)S(1)} %copy-done.2, f32[16,1152]{1,0:T(8,128)S(1)} %copy-done.3, f32[2]{0:T(128)S(1)} %copy-done.5), custom_call_target="tpu_custom_call" | custom-call | tf_op jit(solution)/shard_map/pallas_call | solution.py:577
  90.8 0.6 copy.10
  91.4 0.6 copy.11
Async XLA Ops:
  0.6 0.7 copy-start.4
  0.6 0.7 copy-start.5
  1.3 1.0 %copy-start = (bf16[1152,216]{0,1:T(8,128)(2,1)S(1)}, bf16[1152,216]{0,1:T(8,128)(2,1)}, u32[]{:S(2)}) copy-start(bf16[1152,216]{0,1:T(8,128)(2,1)} %param.8) | copy-start | bytes 1492996
  2.3 0.9 %copy-start.1 = (bf16[16,64,72]{2,1,0:T(8,128)(2,1)S(1)}, bf16[16,64,72]{2,1,0:T(8,128)(2,1)}, u32[]{:S(2)}) copy-start(bf16[16,64,72]{2,1,0:T(8,128)(2,1)} %param.6) | copy-start | bytes 442372
  3.3 0.9 copy-start.2
  4.2 0.9 copy-start.3

commit v3 on v2

--- a/solution.py
+++ b/solution.py
@@ -58,7 +58,7 @@
         gq_out, go_out,
         gat, nrm, img, qt, kt, vt, vtok, prob, wl, live_sc, share_hid,
         part, part_in, pooled_in, grad, outer, sib_out, sib_in, z_out, z_in, acc,
-        y_s, y_r, yf_s, xr_s, xr_r, xl_s, xl_r, fr_s, fr_r, fl_s, fl_r,
+        y_s, y_r, yf_s, xr_s, xr_r, xl_s, xl_r, fr_s, fr_r, fl_s, fl_r, yd_s, yd_r, x2_s, x2_r,
         iy_s, iy_r, ir_s, ir_r, il_s, il_r, is_s, is_r,
         b1_s, b1_r, b2_s, b2_r, c1_s, c1_r, c2_s, c2_r,
     ):
@@ -94,41 +94,18 @@
             )
 
         barrier = pltpu.get_barrier_semaphore()
-        for step in range(1, MP):
-            pl.semaphore_signal(barrier, inc=1, device_id=(dp, (mp + step) % MP), device_id_type=MESH)
-        for p in range(dests - 1):
-            pl.semaphore_signal(barrier, inc=1, device_id=dev_c(p), device_id_type=MESH)
-        pl.semaphore_signal(barrier, inc=1, device_id=sibling, device_id_type=MESH)
+        greeted = [sibling, across]
+        greeted += [(dp, slot(0, k)) for k in range(1, YN)] + [(dp, slot(1, 0)), (dp, slot(-1, 0))]
+        greeted += [dev_z(d) for d in (1, -1, 2, -2)]
+        for device in greeted:
+            pl.semaphore_signal(barrier, inc=1, device_id=device, device_id_type=MESH)
 
         eye_hd = eye(HD)
         for i in range(SUBS):
             gat[i // 2, mp, i % 2] = dot_nt(eye_hd, hid[i * SUB:(i + 1) * SUB, :]).astype(BF16)
         img[z, core, yh] = images[...].astype(BF16)
 
-        count_col = jnp.zeros((CAPS, 1), jnp.int32)
-        row16 = lax.broadcasted_iota(jnp.int32, (CAPS, 1), 0)
-        for c in range(CAPS):
-            count_col = jnp.where(row16 == c, counts[c], count_col)
-        inv_count = 1.0 / count_col.astype(F32)
-        scale_inv = 1.0 / (float(HD) ** 0.5)
-        for i in range(SUBS):
-            caption = lax.broadcasted_iota(jnp.int32, (CAPS, SUB), 0)
-            token = lax.broadcasted_iota(jnp.int32, (CAPS, SUB), 1) + (i * SUB)
-            held = (token // L == caption) & (token % L < count_col)
-            live_sc[i] = held.astype(F32)
-        hid_sum = jnp.zeros((CAPS, HD), F32)
-        for i in range(SUBS):
-            hid_sum = hid_sum + dot_nn(live_sc[i].astype(BF16), hid[i * SUB:(i + 1) * SUB, :])
-        hid_hi, hid_lo = split_two(hid_sum * inv_count)
-        place = (
-            lax.broadcasted_iota(jnp.int32, (HD, D), 1)
-            == lax.broadcasted_iota(jnp.int32, (HD, D), 0) + mp * HD
-        ).astype(F32).astype(BF16)
-        share_hid[...] = dot_nn(hid_hi, place) + dot_nn(hid_lo, place)
-        grad[...] = jnp.zeros_like(grad)
-        outer[...] = jnp.zeros_like(outer)
-
-        pl.semaphore_wait(barrier, MP - 1 + dests - 1 + 1)
+        pl.semaphore_wait(barrier, len(greeted))
 
         def send_y(h, k):
             own = gat.at[h, mp]
@@ -199,6 +176,22 @@
         def recv_fl(h, k):
             block = gat.at[h, slot(2, -k), 1]
             return remote(block, block, fl_s.at[h, k], fl_r.at[h, k], (dp, slot(-1, 0)))
+
+        def send_yd(k):
+            block = gat.at[0, slot(2, 0)]
+            return remote(block, block, yd_s.at[k - 1], yd_r.at[k - 1], (dp, slot(0, k)))
+
+        def recv_yd(k):
+            block = gat.at[0, slot(2, -k)]
+            return remote(block, block, yd_s.at[k - 1], yd_r.at[k - 1], (dp, slot(0, k)))
+
+        def send_x2():
+            block = gat.at[1, slot(0, -k_far)]
+            return remote(block, block, x2_s, x2_r, (dp, slot(2, 0)))
+
+        def recv_x2():
+            block = gat.at[1, slot(2, -k_far)]
+            return remote(block, block, x2_s, x2_r, (dp, slot(2, 0)))
 
         def line(q):
             return yh if q == 0 else 1 - yh
@@ -294,10 +287,48 @@
             recv_xl(h, k).wait_recv()
             send_fl(h, k).start()
 
+        def across_row():
+            recv_fr(0, 0).wait_recv()
+            recv_fl(0, 0).wait_recv()
+            for k in range(1, YN):
+                send_yd(k).start()
+
         def all_in(h):
-            for k in range(YN):
-                recv_fr(h, k).wait_recv()
-                recv_fl(h, k).wait_recv()
+            for n in range(1, YN):
+                if h == 0:
+                    recv_xr(0, order[n]).wait_recv()
+                    recv_xl(0, order[n]).wait_recv()
+                    recv_yd(n).wait_recv()
+                else:
+                    recv_fr(1, order[n - 1]).wait_recv()
+                    recv_fl(1, order[n - 1]).wait_recv()
+            if h == 1:
+                recv_xr(1, k_far).wait_recv()
+                recv_xl(1, k_far).wait_recv()
+                recv_x2().wait_recv()
+
+        count_col = jnp.zeros((CAPS, 1), jnp.int32)
+        row16 = lax.broadcasted_iota(jnp.int32, (CAPS, 1), 0)
+        for c in range(CAPS):
+            count_col = jnp.where(row16 == c, counts[c], count_col)
+        inv_count = 1.0 / count_col.astype(F32)
+        scale_inv = 1.0 / (float(HD) ** 0.5)
+        for i in range(SUBS):
+            caption = lax.broadcasted_iota(jnp.int32, (CAPS, SUB), 0)
+            token = lax.broadcasted_iota(jnp.int32, (CAPS, SUB), 1) + (i * SUB)
+            held = (token // L == caption) & (token % L < count_col)
+            live_sc[i] = held.astype(F32)
+        hid_sum = jnp.zeros((CAPS, HD), F32)
+        for i in range(SUBS):
+            hid_sum = hid_sum + dot_nn(live_sc[i].astype(BF16), hid[i * SUB:(i + 1) * SUB, :])
+        hid_hi, hid_lo = split_two(hid_sum * inv_count)
+        place = (
+            lax.broadcasted_iota(jnp.int32, (HD, D), 1)
+            == lax.broadcasted_iota(jnp.int32, (HD, D), 0) + mp * HD
+        ).astype(F32).astype(BF16)
+        share_hid[...] = dot_nn(hid_hi, place) + dot_nn(hid_lo, place)
+        grad[...] = jnp.zeros_like(grad)
+        outer[...] = jnp.zeros_like(outer)
 
         def forward_sub(h, s):
             i = h * 2 + s
@@ -332,27 +363,26 @@
                 prob[i, b] = probs
                 wl[i, :, lanes] = dot_nt(live_here[:, lanes], probs.astype(BF16))
 
-        for n in range(1, YN):
-            y_to_x(0, n)
+        y_to_x(0, 1)
         pass_on(0, 0)
+        y_to_x(0, 2)
         image_step(0, 2)
+        pass_on(1, 0)
+        image_step(1, 1)
         y_to_x(1, 1)
-        pass_on(0, 1)
-        image_step(1, 1)
+        across_row()
+        y_to_x(0, 3)
         y_to_x(1, 2)
-        pass_on(0, 2)
+        image_step(0, 3)
+        image_step(1, 2)
         y_to_x(1, 3)
-        pass_on(0, 3)
-        image_step(0, 3)
-        pass_on(1, 0)
-        image_step(1, 2)
+        send_x2().start()
         pass_on(1, 1)
+        pass_on(1, 2)
+        all_in(0)
+        forward_sub(0, 0)
         for step in range(4, last_step + 1):
             image_step(0, step)
-        pass_on(1, 2)
-        pass_on(1, 3)
-        all_in(0)
-        forward_sub(0, 0)
         image_step(1, 3)
         forward_sub(0, 1)
         all_in(1)
@@ -537,8 +567,12 @@
             for k in range(YN):
                 send_xr(h, k).wait_send()
                 send_xl(h, k).wait_send()
-                send_fr(h, k).wait_send()
-                send_fl(h, k).wait_send()
+        for h, n in ((0, 0), (1, 0), (1, 1), (1, 2)):
+            send_fr(h, order[n]).wait_send()
+            send_fl(h, order[n]).wait_send()
+        for k in range(1, YN):
+            send_yd(k).wait_send()
+        send_x2().wait_send()
         send_iy().wait_send()
         for q in range(2):
             for d in range(1, right_most + 1):
@@ -607,6 +641,7 @@
                 dma((2, YN - 1)), dma((2, YN - 1)), dma((2,)),
                 dma((2, YN)), dma((2, YN)), dma((2, YN)), dma((2, YN)),
                 dma((2, YN)), dma((2, YN)), dma((2, YN)), dma((2, YN)),
+                dma((YN - 1,)), dma((YN - 1,)), dma, dma,
                 dma, dma,
                 dma((2, right_most)), dma((2, right_most)), dma((2, left_most)), dma((2, left_most)),
                 dma((2, zn)), dma((2, zn)),

time: 92.3 us -> 89.2 us (0.966)
  Pallas kernels: 85.7 us -> 82.3 us
    pallas_call x1, Pallas kernels: 85.7 us -> 82.3 us  [on_device(): pl.pallas_call(make_kernel(zn), out_shape=(jax.ShapeDtypeStruct((OWN, 3 *...]
where the time goes in v3:
time: 89.2 us; the launch traced here: 88.6 us
  Pallas kernels  82.3 us (92%)
  local copies, waits for them, and re-layouts  5.65 us (6%)
    pallas_call x1, Pallas kernels, on_device(): pl.pallas_call(make_kernel(zn), out_shape=(jax.ShapeDtypeStruct((OWN, 3 *...  82.3 us
    unnamed x14, local copies, waits for them, and re-layouts  5.65 us

profile of v3, /device:TPU:1, one launch (start us, length us, event | category | flops | bytes accessed | tf_op | source)
XLA Modules:
  0.0 88.6 jit_solution(12427995254842649509)
XLA Ops:
  0.6 0.0 copy-start.4
  0.6 0.0 copy-start.5
  0.7 0.6 copy-done.4
  1.3 0.0 copy-done.5
  1.3 0.0 copy-start
  1.3 1.0 %copy-done = bf16[1152,216]{0,1:T(8,128)(2,1)S(1)} copy-done((bf16[1152,216]{0,1:T(8,128)(2,1)S(1)}, bf16[1152,216]{0,1:T(8,128)(2,1)}, u32[]{:S(2)}) %copy-start) | copy-done | bytes 497688
  2.3 0.0 copy-start.1
  2.3 0.9 %copy-done.1 = bf16[16,64,72]{2,1,0:T(8,128)(2,1)S(1)} copy-done((bf16[16,64,72]{2,1,0:T(8,128)(2,1)S(1)}, bf16[16,64,72]{2,1,0:T(8,128)(2,1)}, u32[]{:S(2)}) %copy-start.1) | copy-done | bytes 147480
  3.3 0.0 copy-start.2
  3.3 0.9 %copy-done.2 = bf16[72,1152]{1,0:T(8,128)(2,1)S(1)} copy-done((bf16[72,1152]{1,0:T(8,128)(2,1)S(1)}, bf16[72,1152]{1,0:T(8,128)(2,1)}, u32[]{:S(2)}) %copy-start.2) | copy-done | bytes 165912
  4.2 0.0 copy-start.3
  4.2 0.9 copy-done.3
  5.1 82.3 %shard_map.77 = (f32[24,216]{1,0:T(8,128)S(1)}, f32[24,72]{1,0:T(8,128)S(1)}) custom-call(bf16[1024,72]{1,0:T(8,128)(2,1)S(1)} %bitcast.4, s32[16]{0:T(128)S(1)} %copy-done.4, bf16[216,1152]{1,0:T(8,128)(2,1)S(1)} %bitcast.3, bf16[72,1152]{1,0:T(8,128)(2,1)S(1)} %copy-done.2, f32[16,1152]{1,0:T(8,128)S(1)} %copy-done.3, f32[2]{0:T(128)S(1)} %copy-done.5), custom_call_target="tpu_custom_call" | custom-call | tf_op jit(solution)/shard_map/pallas_call | solution.py:611
  87.4 0.6 copy.10
  88.0 0.6 copy.11
Async XLA Ops:
  0.6 0.7 copy-start.4
  0.6 0.7 copy-start.5
  1.3 1.0 %copy-start = (bf16[1152,216]{0,1:T(8,128)(2,1)S(1)}, bf16[1152,216]{0,1:T(8,128)(2,1)}, u32[]{:S(2)}) copy-start(bf16[1152,216]{0,1:T(8,128)(2,1)} %param.8) | copy-start | bytes 1492996
  2.3 0.9 %copy-start.1 = (bf16[16,64,72]{2,1,0:T(8,128)(2,1)S(1)}, bf16[16,64,72]{2,1,0:T(8,128)(2,1)}, u32[]{:S(2)}) copy-start(bf16[16,64,72]{2,1,0:T(8,128)(2,1)} %param.6) | copy-start | bytes 442372
  3.3 0.9 %copy-start.2 = (bf16[72,1152]{1,0:T(8,128)(2,1)S(1)}, bf16[72,1152]{1,0:T(8,128)(2,1)}, u32[]{:S(2)}) copy-start(bf16[72,1152]{1,0:T(8,128)(2,1)} %w_out.1) | copy-start | bytes 497668
  4.2 0.9 copy-start.3

commit v4 on v3

--- a/solution.py
+++ b/solution.py
@@ -18,6 +18,7 @@
 OWN = 24
 ROWS = 32
 GROUPS = 3
+REACH = 3
 SLICES = D // 128
 
 MESH = pl.DeviceIdType.MESH
@@ -58,7 +59,7 @@
         gq_out, go_out,
         gat, nrm, img, qt, kt, vt, vtok, prob, wl, live_sc, share_hid,
         part, part_in, pooled_in, grad, outer, sib_out, sib_in, z_out, z_in, acc,
-        y_s, y_r, yf_s, xr_s, xr_r, xl_s, xl_r, fr_s, fr_r, fl_s, fl_r, yd_s, yd_r, x2_s, x2_r,
+        y_s, y_r, yf_s, xr_s, xr_r, xl_s, xl_r, fr_s, fr_r, fl_s, fl_r, yd_s, yd_r,
         iy_s, iy_r, ir_s, ir_r, il_s, il_r, is_s, is_r,
         b1_s, b1_r, b2_s, b2_r, c1_s, c1_r, c2_s, c2_r,
     ):
@@ -96,7 +97,7 @@
         barrier = pltpu.get_barrier_semaphore()
         greeted = [sibling, across]
         greeted += [(dp, slot(0, k)) for k in range(1, YN)] + [(dp, slot(1, 0)), (dp, slot(-1, 0))]
-        greeted += [dev_z(d) for d in (1, -1, 2, -2)]
+        greeted += [dev_z(d) for d in (1, -1, 2, -2, 3, -3)]
         for device in greeted:
             pl.semaphore_signal(barrier, inc=1, device_id=device, device_id_type=MESH)
 
@@ -177,21 +178,13 @@
             block = gat.at[h, slot(2, -k), 1]
             return remote(block, block, fl_s.at[h, k], fl_r.at[h, k], (dp, slot(-1, 0)))
 
-        def send_yd(k):
-            block = gat.at[0, slot(2, 0)]
-            return remote(block, block, yd_s.at[k - 1], yd_r.at[k - 1], (dp, slot(0, k)))
-
-        def recv_yd(k):
-            block = gat.at[0, slot(2, -k)]
-            return remote(block, block, yd_s.at[k - 1], yd_r.at[k - 1], (dp, slot(0, k)))
-
-        def send_x2():
-            block = gat.at[1, slot(0, -k_far)]
-            return remote(block, block, x2_s, x2_r, (dp, slot(2, 0)))
-
-        def recv_x2():
-            block = gat.at[1, slot(2, -k_far)]
-            return remote(block, block, x2_s, x2_r, (dp, slot(2, 0)))
+        def send_yd(h, k):
+            block = gat.at[h, slot(2, 0)]
+            return remote(block, block, yd_s.at[h, k - 1], yd_r.at[h, k - 1], (dp, slot(0, k)))
+
+        def recv_yd(h, k):
+            block = gat.at[h, slot(2, -k)]
+            return remote(block, block, yd_s.at[h, k - 1], yd_r.at[h, k - 1], (dp, slot(0, k)))
 
         def line(q):
             return yh if q == 0 else 1 - yh
@@ -205,7 +198,7 @@
             return remote(got, got, iy_s, iy_r, across)
 
         def send_ir(q, d):
-            reach = 2 - d % 2
+            reach = (d - 1) % REACH + 1
             block = img.at[at_z(reach - d), core, line(q)]
             return remote(block, block, ir_s.at[q, d - 1], ir_r.at[q, d - 1], dev_z(reach))
 
@@ -214,7 +207,7 @@
             return remote(block, block, ir_s.at[q, d - 1], ir_r.at[q, d - 1], dev_z(1))
 
         def send_il(q, d):
-            reach = 2 - d % 2
+            reach = (d - 1) % REACH + 1
             block = img.at[at_z(d - reach), core, line(q)]
             return remote(block, block, il_s.at[q, d - 1], il_r.at[q, d - 1], dev_z(-reach))
 
@@ -232,36 +225,35 @@
             n = (s + zn) % zn
             return remote(block, block, is_s.at[q, n], is_r.at[q, n], sibling)
 
+        def reach_out(q, first):
+            for d in range(first + REACH - 1, first - 1, -1):
+                if d <= right_most:
+                    send_ir(q, d).start()
+                if d <= left_most:
+                    send_il(q, d).start()
+
         def image_step(q, step):
-            near, far = 2 * step - 3, 2 * step - 2
             if step == 1:
                 if q == 1:
                     recv_iy().wait_recv()
-            else:
-                for d in (far, near):
-                    if d <= right_most:
-                        recv_ir(q, d).wait_recv()
-                    if d <= left_most:
-                        recv_il(q, d).wait_recv()
-                    if d == far and d + 1 <= right_most:
-                        send_ir(q, d + 1).start()
-                        if d + 2 <= right_most:
-                            send_ir(q, d + 2).start()
-                    if d == far and d + 1 <= left_most:
-                        send_il(q, d + 1).start()
-                        if d + 2 <= left_most:
-                            send_il(q, d + 2).start()
-                    if d <= right_most:
-                        send_is(q, -d).start()
-                    if d <= left_most:
-                        send_is(q, d).start()
-            if step == 1:
-                for d in (2, 1):
-                    send_ir(q, d).start()
-                    send_il(q, d).start()
+                reach_out(q, 1)
                 send_is(q, 0).start()
-
-        last_step = (right_most + 1) // 2 + 1
+                return
+            far = (step - 1) * REACH
+            for d in range(far, far - REACH, -1):
+                if d <= right_most:
+                    recv_ir(q, d).wait_recv()
+                if d <= left_most:
+                    recv_il(q, d).wait_recv()
+                if d == far:
+                    reach_out(q, d + 1)
+            for d in range(far - REACH + 1, far + 1):
+                if d <= right_most:
+                    send_is(q, -d).start()
+                if d <= left_most:
+                    send_is(q, d).start()
+
+        last_step = (right_most + REACH - 1) // REACH + 1
 
         each_y(0, lambda c: c.start())
         send_xr(0, 0).start()
@@ -287,25 +279,17 @@
             recv_xl(h, k).wait_recv()
             send_fl(h, k).start()
 
-        def across_row():
-            recv_fr(0, 0).wait_recv()
-            recv_fl(0, 0).wait_recv()
+        def across_row(h):
+            recv_fr(h, 0).wait_recv()
+            recv_fl(h, 0).wait_recv()
             for k in range(1, YN):
-                send_yd(k).start()
+                send_yd(h, k).start()
 
         def all_in(h):
             for n in range(1, YN):
-                if h == 0:
-                    recv_xr(0, order[n]).wait_recv()
-                    recv_xl(0, order[n]).wait_recv()
-                    recv_yd(n).wait_recv()
-                else:
-                    recv_fr(1, order[n - 1]).wait_recv()
-                    recv_fl(1, order[n - 1]).wait_recv()
-            if h == 1:
-                recv_xr(1, k_far).wait_recv()
-                recv_xl(1, k_far).wait_recv()
-                recv_x2().wait_recv()
+                recv_xr(h, order[n]).wait_recv()
+                recv_xl(h, order[n]).wait_recv()
+                recv_yd(h, n).wait_recv()
 
         count_col = jnp.zeros((CAPS, 1), jnp.int32)
         row16 = lax.broadcasted_iota(jnp.int32, (CAPS, 1), 0)
@@ -366,24 +350,18 @@
         y_to_x(0, 1)
         pass_on(0, 0)
         y_to_x(0, 2)
-        image_step(0, 2)
         pass_on(1, 0)
         image_step(1, 1)
         y_to_x(1, 1)
-        across_row()
+        across_row(0)
         y_to_x(0, 3)
+        across_row(1)
         y_to_x(1, 2)
-        image_step(0, 3)
+        image_step(0, 2)
+        y_to_x(1, 3)
         image_step(1, 2)
-        y_to_x(1, 3)
-        send_x2().start()
-        pass_on(1, 1)
-        pass_on(1, 2)
         all_in(0)
         forward_sub(0, 0)
-        for step in range(4, last_step + 1):
-            image_step(0, step)
-        image_step(1, 3)
         forward_sub(0, 1)
         all_in(1)
         forward_sub(1, 0)
@@ -418,9 +396,6 @@
             def _():
                 send_b1(j).start()
 
-        for step in range(4, last_step + 1):
-            image_step(1, step)
-
         @pl.when(mp < SLICES)
         def _():
             total = part[mp]
@@ -431,6 +406,9 @@
             for step in range(1, MP):
                 send_b2(step).start()
 
+        for step in range(3, last_step + 1):
+            for q in range(2):
+                image_step(q, step)
         for q in range(2):
             for s in range(zn):
                 recv_is(q, s).wait_recv()
@@ -567,12 +545,10 @@
             for k in range(YN):
                 send_xr(h, k).wait_send()
                 send_xl(h, k).wait_send()
-        for h, n in ((0, 0), (1, 0), (1, 1), (1, 2)):
-            send_fr(h, order[n]).wait_send()
-            send_fl(h, order[n]).wait_send()
-        for k in range(1, YN):
-            send_yd(k).wait_send()
-        send_x2().wait_send()
+            send_fr(h, 0).wait_send()
+            send_fl(h, 0).wait_send()
+            for k in range(1, YN):
+                send_yd(h, k).wait_send()
         send_iy().wait_send()
         for q in range(2):
             for d in range(1, right_most + 1):
@@ -641,7 +617,7 @@
                 dma((2, YN - 1)), dma((2, YN - 1)), dma((2,)),
                 dma((2, YN)), dma((2, YN)), dma((2, YN)), dma((2, YN)),
                 dma((2, YN)), dma((2, YN)), dma((2, YN)), dma((2, YN)),
-                dma((YN - 1,)), dma((YN - 1,)), dma, dma,
+                dma((2, YN - 1)), dma((2, YN - 1)),
                 dma, dma,
                 dma((2, right_most)), dma((2, right_most)), dma((2, left_most)), dma((2, left_most)),
                 dma((2, zn)), dma((2, zn)),

time: 89.2 us -> 88.4 us (level)
  no operation moved by 1% of the time
where the time goes in v4:
time: 88.4 us; the launch traced here: 88.1 us
  Pallas kernels  81.8 us (93%)
  local copies, waits for them, and re-layouts  5.65 us (6%)
    pallas_call x1, Pallas kernels, on_device(): pl.pallas_call(make_kernel(zn), out_shape=(jax.ShapeDtypeStruct((OWN, 3 *...  81.8 us
    unnamed x14, local copies, waits for them, and re-layouts  5.65 us

profile of v4, /device:TPU:1, one launch (start us, length us, event | category | flops | bytes accessed | tf_op | source)
XLA Modules:
  0.0 88.1 jit_solution(11561656670402967668)
XLA Ops:
  0.6 0.0 copy-start.4
  0.6 0.0 copy-start.5
  0.7 0.6 copy-done.4
  1.3 0.0 copy-done.5
  1.3 0.0 copy-start
  1.3 1.0 %copy-done = bf16[1152,216]{0,1:T(8,128)(2,1)S(1)} copy-done((bf16[1152,216]{0,1:T(8,128)(2,1)S(1)}, bf16[1152,216]{0,1:T(8,128)(2,1)}, u32[]{:S(2)}) %copy-start) | copy-done | bytes 497688
  2.3 0.0 copy-start.1
  2.3 0.9 %copy-done.1 = bf16[16,64,72]{2,1,0:T(8,128)(2,1)S(1)} copy-done((bf16[16,64,72]{2,1,0:T(8,128)(2,1)S(1)}, bf16[16,64,72]{2,1,0:T(8,128)(2,1)}, u32[]{:S(2)}) %copy-start.1) | copy-done | bytes 147480
  3.3 0.0 copy-start.2
  3.3 0.9 %copy-done.2 = bf16[72,1152]{1,0:T(8,128)(2,1)S(1)} copy-done((bf16[72,1152]{1,0:T(8,128)(2,1)S(1)}, bf16[72,1152]{1,0:T(8,128)(2,1)}, u32[]{:S(2)}) %copy-start.2) | copy-done | bytes 165912
  4.2 0.0 copy-start.3
  4.2 0.9 %copy-done.3 = f32[16,1152]{1,0:T(8,128)S(1)} copy-done((f32[16,1152]{1,0:T(8,128)S(1)}, f32[16,1152]{1,0:T(8,128)}, u32[]{:S(2)}) %copy-start.3) | copy-done | bytes 73752
  5.1 81.8 %shard_map.77 = (f32[24,216]{1,0:T(8,128)S(1)}, f32[24,72]{1,0:T(8,128)S(1)}) custom-call(bf16[1024,72]{1,0:T(8,128)(2,1)S(1)} %bitcast.4, s32[16]{0:T(128)S(1)} %copy-done.4, bf16[216,1152]{1,0:T(8,128)(2,1)S(1)} %bitcast.3, bf16[72,1152]{1,0:T(8,128)(2,1)S(1)} %copy-done.2, f32[16,1152]{1,0:T(8,128)S(1)} %copy-done.3, f32[2]{0:T(128)S(1)} %copy-done.5), custom_call_target="tpu_custom_call" | custom-call | tf_op jit(solution)/shard_map/pallas_call | solution.py:587
  86.9 0.6 copy.10
  87.5 0.6 copy.11
Async XLA Ops:
  0.6 0.7 copy-start.4
  0.6 0.7 copy-start.5
  1.3 1.0 %copy-start = (bf16[1152,216]{0,1:T(8,128)(2,1)S(1)}, bf16[1152,216]{0,1:T(8,128)(2,1)}, u32[]{:S(2)}) copy-start(bf16[1152,216]{0,1:T(8,128)(2,1)} %param.8) | copy-start | bytes 1492996
  2.3 0.9 %copy-start.1 = (bf16[16,64,72]{2,1,0:T(8,128)(2,1)S(1)}, bf16[16,64,72]{2,1,0:T(8,128)(2,1)}, u32[]{:S(2)}) copy-start(bf16[16,64,72]{2,1,0:T(8,128)(2,1)} %param.6) | copy-start | bytes 442372
  3.3 0.9 %copy-start.2 = (bf16[72,1152]{1,0:T(8,128)(2,1)S(1)}, bf16[72,1152]{1,0:T(8,128)(2,1)}, u32[]{:S(2)}) copy-start(bf16[72,1152]{1,0:T(8,128)(2,1)} %w_out.1) | copy-start | bytes 497668
  4.2 0.9 %copy-start.3 = (f32[16,1152]{1,0:T(8,128)S(1)}, f32[16,1152]{1,0:T(8,128)}, u32[]{:S(2)}) copy-start(f32[16,1152]{1,0:T(8,128)} %images.1) | copy-start | bytes 221188
